TPU v7x, 128 devices: a whole 4x4x4 slice. The times are simulated.
128 devices in a mesh: range: 4 (over z_hi, core), azimuth: 32 (over x, y, z_lo).
Axes of the slice: x: 4, y: 4, z: 4 (z_hi: 2, z_lo: 2; z = z_hi * 2 + z_lo), core: 2. Of those that a mesh axis runs over, the one named last changes fastest.
Arguments:
- features: bfloat16 [4, 64, 64, 4096], P(None, None, 'range', 'azimuth'), may hold values from -6 to 6
- state_init: bfloat16 [64, 64, 4096], P(None, 'range', 'azimuth'), may hold values from -3 to 3
- kernel: float32 [64, 3, 3], replicated, may hold values from -2 to 2
- gate_weight: bfloat16 [128, 128], replicated, may hold values from -0.5 to 0.5
- cand_weight: bfloat16 [64, 64], replicated, may hold values from -0.75 to 0.75
- recur_weight: bfloat16 [64, 64], replicated, may hold values from -0.75 to 0.75
- down_weight: bfloat16 [128, 1024], replicated, may hold values from -0.1875 to 0.1875
- owner_map: int32 [4, 32, 4], P('range', 'azimuth'), may hold values from 0 to 3, as said below
- dest_map: int32 [4, 32, 4], P('range', 'azimuth'), may hold values from 0 to 3
- cart_cot: bfloat16 [4, 32, 4, 128, 128], P('range', 'azimuth'), may hold values from -6 to 6
Outputs:
- cart: float32 [4, 32, 4, 128, 128], P('range', 'azimuth')
- grad_features: bfloat16 [4, 64, 64, 4096], P(None, None, 'range', 'azimuth')
- grad_state: float32 [64, 64, 4096], P(None, 'range', 'azimuth')
- grad_kernel: float32 [64, 3, 3], replicated
- grad_gate: float32 [128, 128], replicated
- grad_cand: float32 [64, 64], replicated
- grad_recur: float32 [64, 64], replicated
- grad_down: float32 [128, 1024], replicated
Inputs may be any that keep to these rules, and one draw needn't show every extreme that they name: `owner_map`: no tile sends more than 2 of its 4 blocks to one owner; in every azimuth column one owner receives exactly 2 blocks from every tile of the column.
All inputs are finite; a program needn't handle non-finite values.
Results may differ from a plain program's by a relative error of at most 0.0065.
Values may be sent and summed in bfloat16 or wider, within the bound.
A program may use at most 128 MiB of HBM per device.

v0:
```python
import math

import jax
import jax.numpy as jnp
from jax import lax
from jax.sharding import PartitionSpec as P

DILATION = 8


def extended(block, sides, width, periodic):
    for axis, dim in sides:
        count = lax.axis_size(axis)
        forward = [(i, i + 1) for i in range(count - 1)]
        if periodic:
            forward.append((count - 1, 0))
        backward = [(target, source) for source, target in forward]
        low = lax.ppermute(
            lax.slice_in_dim(block, block.shape[dim] - width, None, axis=dim), axis, forward
        )
        high = lax.ppermute(lax.slice_in_dim(block, 0, width, axis=dim), axis, backward)
        block = jnp.concatenate([low, block, high], axis=dim)
    return block


def depthwise(padded, kernel, tile_rows, tile_cols):
    summed = jnp.zeros((padded.shape[0], tile_rows, tile_cols), jnp.float32)
    for tap_row in range(3):
        for tap_col in range(3):
            window = padded[
                :,
                tap_row : tap_row + tile_rows,
                tap_col * DILATION : tap_col * DILATION + tile_cols,
            ]
            summed = summed + kernel[:, tap_row, tap_col][:, None, None] * window.astype(
                jnp.float32
            )
    return summed


def kernel_terms(padded, dconv, tile_rows, tile_cols):
    grads = dconv.astype(jnp.float32)
    outer_rows = []
    for tap_row in range(3):
        inner_cols = []
        for tap_col in range(3):
            window = padded[
                :,
                tap_row : tap_row + tile_rows,
                tap_col * DILATION : tap_col * DILATION + tile_cols,
            ]
            inner_cols.append(jnp.sum(grads * window.astype(jnp.float32), axis=(1, 2)))
        outer_rows.append(jnp.stack(inner_cols, axis=1))
    return jnp.stack(outer_rows, axis=1)


def patches(values, tile_rows, tile_cols):
    channels = values.shape[0]
    shaped = values.reshape(channels, tile_rows // 4, 4, tile_cols // 4, 4).transpose(0, 2, 4, 1, 3)
    return shaped.reshape(16 * channels, tile_rows * tile_cols // 16)


def unpatches(grads, tile_rows, tile_cols):
    channels = grads.shape[0] // 16
    shaped = grads.reshape(channels, 4, 4, tile_rows // 4, tile_cols // 4).transpose(0, 3, 1, 4, 2)
    return shaped.reshape(channels, tile_rows * tile_cols)


def cross_cells(left, right):
    return lax.dot_general(
        left, right, (((1,), (1,)), ((), ())), preferred_element_type=jnp.float32
    )


def back_product(weight, grads):
    return lax.dot_general(
        weight, grads, (((0,), (0,)), ((), ())), preferred_element_type=jnp.float32
    )


def cell_gates(conv_bf, prior_bf, gate_weight, cand_weight, recur_weight):
    channels = conv_bf.shape[0]
    stacked = jnp.concatenate([conv_bf, prior_bf], axis=0)
    preact = jnp.dot(gate_weight, stacked, preferred_element_type=jnp.float32)
    update = jax.nn.sigmoid(preact[:channels])
    reset = jax.nn.sigmoid(preact[channels:])
    recurrent = jnp.dot(recur_weight, prior_bf, preferred_element_type=jnp.float32)
    candidate = jnp.tanh(
        jnp.dot(cand_weight, conv_bf, preferred_element_type=jnp.float32) + reset * recurrent
    )
    return (stacked, update, reset, recurrent, candidate)


def reverse_cell(
    flow_grad,
    prior_state,
    update,
    reset,
    recurrent,
    candidate,
    gate_weight,
    cand_weight,
    recur_weight,
):
    channels = update.shape[0]
    d_update = flow_grad * (candidate - prior_state)
    d_act = flow_grad * update * (1.0 - candidate * candidate)
    d_recur = d_act * reset
    gate_delta = jnp.concatenate(
        [d_update * update * (1.0 - update), d_act * recurrent * reset * (1.0 - reset)], axis=0
    ).astype(jnp.bfloat16)
    cand_delta = d_act.astype(jnp.bfloat16)
    recur_delta = d_recur.astype(jnp.bfloat16)
    reverse_in = back_product(gate_weight, gate_delta)
    dconv = (reverse_in[:channels] + back_product(cand_weight, cand_delta)).astype(jnp.bfloat16)
    carry = (
        (1.0 - update) * flow_grad + reverse_in[channels:] + back_product(recur_weight, recur_delta)
    )
    return (carry, dconv, gate_delta, cand_delta, recur_delta)


def framed_each(field):
    taller = extended(field, (("range", 2),), 1, False)
    return extended(taller, (("azimuth", 3),), DILATION, True)


def on_device(
    features,
    state_init,
    kernel,
    gate_weight,
    cand_weight,
    recur_weight,
    down_weight,
    owner_map,
    dest_map,
    cart_cot,
):
    slice_count, channels, tile_rows, tile_cols = features.shape
    cell_count = tile_rows * tile_cols
    coarse_ch = down_weight.shape[0]
    rank_count = lax.axis_size("range")
    block_count = owner_map.shape[2]
    per_slice = block_count // slice_count
    block_cells = cell_count // 16 // per_slice
    capacity = block_count // 2
    hidden = state_init.reshape(channels, cell_count).astype(jnp.float32)
    padded_list = []
    conv_list = []
    hidden_list = [hidden]
    block_list = []
    for instant in range(slice_count):
        padded = framed_each(features[instant][None])[0]
        conv_bf = (
            depthwise(padded, kernel, tile_rows, tile_cols)
            .astype(jnp.bfloat16)
            .reshape(channels, cell_count)
        )
        stacked, update, reset, recurrent, candidate = cell_gates(
            conv_bf, hidden.astype(jnp.bfloat16), gate_weight, cand_weight, recur_weight
        )
        hidden = (1.0 - update) * hidden + update * candidate
        coarse = jnp.dot(
            down_weight,
            patches(hidden.astype(jnp.bfloat16), tile_rows, tile_cols),
            preferred_element_type=jnp.float32,
        ).astype(jnp.bfloat16)
        block_list.append(coarse.reshape(coarse_ch, per_slice, block_cells).transpose(1, 0, 2))
        padded_list.append(padded)
        conv_list.append(conv_bf)
        hidden_list.append(hidden)
    blocks = jnp.concatenate(block_list, axis=0).reshape(block_count, coarse_ch * block_cells)
    owners = owner_map[0, 0]
    targets = dest_map[0, 0]
    matches = (owners[None, :] == jnp.arange(rank_count, dtype=jnp.int32)[:, None]).astype(
        jnp.int32
    )
    position = jnp.cumsum(matches, axis=1) - matches
    picks = (matches[:, None, :] == 1) & (
        position[:, None, :] == jnp.arange(capacity, dtype=jnp.int32)[None, :, None]
    )
    pick_flat = picks.reshape(rank_count * capacity, block_count)
    outgoing = jnp.dot(
        pick_flat.astype(jnp.bfloat16), blocks, preferred_element_type=jnp.float32
    ).astype(jnp.bfloat16)
    outgoing = outgoing.reshape(rank_count, capacity, coarse_ch * block_cells)
    labels = jnp.sum(picks.astype(jnp.int32) * (targets[None, None, :] + 1), axis=2)
    arrived, arrived_labels = (
        lax.all_to_all(outgoing, "range", split_axis=0, concat_axis=0, tiled=True),
        lax.all_to_all(labels, "range", split_axis=0, concat_axis=0, tiled=True),
    )
    landing = (
        arrived_labels.reshape(1, rank_count * capacity) - 1
        == jnp.arange(block_count, dtype=jnp.int32)[:, None]
    ).astype(jnp.bfloat16)
    cartesian = jnp.dot(
        landing,
        arrived.reshape(rank_count * capacity, coarse_ch * block_cells),
        preferred_element_type=jnp.float32,
    )
    cartesian = cartesian.reshape(1, 1, block_count, coarse_ch, block_cells)
    cot_flat = cart_cot.reshape(block_count, coarse_ch * block_cells)
    replies = (
        back_product(landing, cot_flat)
        .astype(jnp.bfloat16)
        .reshape(rank_count, capacity, coarse_ch * block_cells)
    )
    returned = lax.all_to_all(replies, "range", split_axis=0, concat_axis=0, tiled=True)
    backed = back_product(
        pick_flat.astype(jnp.bfloat16),
        returned.reshape(rank_count * capacity, coarse_ch * block_cells),
    ).astype(jnp.bfloat16)
    carry = jnp.zeros((channels, cell_count), jnp.float32)
    grad_kernel = jnp.zeros((channels, 3, 3), jnp.float32)
    grad_gate = jnp.zeros((2 * channels, 2 * channels), jnp.float32)
    grad_cand = jnp.zeros((channels, channels), jnp.float32)
    grad_recur = jnp.zeros((channels, channels), jnp.float32)
    grad_down = jnp.zeros((coarse_ch, 16 * channels), jnp.float32)
    grad_list = [None] * slice_count
    flipped = kernel[:, ::-1, ::-1]
    for instant in range(slice_count - 1, -1, -1):
        prior_state = hidden_list[instant]
        prior_bf = prior_state.astype(jnp.bfloat16)
        conv_bf = conv_list[instant]
        stacked, update, reset, recurrent, candidate = cell_gates(
            conv_bf, prior_bf, gate_weight, cand_weight, recur_weight
        )
        next_bf = hidden_list[instant + 1].astype(jnp.bfloat16)
        slice_blocks = backed[instant * per_slice : (instant + 1) * per_slice].reshape(
            per_slice, coarse_ch, block_cells
        )
        d_coarse = slice_blocks.transpose(1, 0, 2).reshape(coarse_ch, per_slice * block_cells)
        grad_down = grad_down + cross_cells(d_coarse, patches(next_bf, tile_rows, tile_cols))
        flow_grad = carry + unpatches(back_product(down_weight, d_coarse), tile_rows, tile_cols)
        carry, dconv, gate_delta, cand_delta, recur_delta = reverse_cell(
            flow_grad,
            prior_state,
            update,
            reset,
            recurrent,
            candidate,
            gate_weight,
            cand_weight,
            recur_weight,
        )
        grad_gate = grad_gate + cross_cells(gate_delta, stacked)
        grad_cand = grad_cand + cross_cells(cand_delta, conv_bf)
        grad_recur = grad_recur + cross_cells(recur_delta, prior_bf)
        dconv_grid = dconv.reshape(channels, tile_rows, tile_cols)
        grad_kernel = grad_kernel + kernel_terms(
            padded_list[instant], dconv_grid, tile_rows, tile_cols
        )
        dpadded = framed_each(dconv_grid[None])[0]
        grad_list[instant] = depthwise(dpadded, flipped, tile_rows, tile_cols).astype(jnp.bfloat16)
    grad_kernel, grad_gate, grad_cand, grad_recur, grad_down = lax.psum(
        (grad_kernel, grad_gate, grad_cand, grad_recur, grad_down), ("range", "azimuth")
    )
    grad_scale = 1.0 / math.sqrt(slice_count * cell_count * rank_count * lax.axis_size("azimuth"))
    grad_features = jnp.stack(grad_list, axis=0)
    grad_state = carry.reshape(channels, tile_rows, tile_cols)
    return (
        cartesian,
        grad_features,
        grad_state,
        grad_kernel * grad_scale,
        grad_gate * grad_scale,
        grad_cand * grad_scale,
        grad_recur * grad_scale,
        grad_down * grad_scale,
    )


def solution(mesh):
    placed = (
        P(None, None, "range", "azimuth"),
        P(None, "range", "azimuth"),
        P(),
        P(),
        P(),
        P(),
        P(),
        P("range", "azimuth", None),
        P("range", "azimuth", None),
        P("range", "azimuth", None, None, None),
    )
    return jax.shard_map(
        on_device,
        mesh=mesh,
        in_specs=placed,
        out_specs=(
            P("range", "azimuth", None, None, None),
            P(None, None, "range", "azimuth"),
            P(None, "range", "azimuth"),
            P(),
            P(),
            P(),
            P(),
            P(),
        ),
        check_vma=False,
    )
```

profile of v0, /device:TPU:1, one launch (start us, length us, event | category | flops | bytes accessed | tf_op | source)
XLA Modules:
  0.0 565.9 jit_solution(10220124588533792842)
XLA Ops:
  10.2 6.6 %all-to-all-start = ((s32[4,1,2]{2,1,0:T(1,128)}), s32[4,1,2]{2,1,0:T(1,128)S(1)}, u32[]{:S(2)}, u32[]{:S(2)}) async-start(s32[4,1,2]{2,1,0:T(1,128)} %bitcast.126), calls=%async_computation | async-start | bytes 4096 | tf_op jit(solution)/shard_map/all_to_all | solution.py:190
  19.0 5.2 collective-permute-start.12
  26.1 5.1 collective-permute-start.8
  33.1 5.1 collective-permute-start
  49.8 5.1 collective-permute-start.4
  59.8 4.9 collective-permute-start.7
  64.8 5.7 %collective-permute-start.3 = (bf16[1,64,18,8]{3,2,1,0:T(8,128)(2,1)S(1)}, bf16[1,64,18,8]{3,2,1,0:T(8,128)(2,1)S(1)}, u32[]{:S(2)}, u32[]{:S(2)}) collective-permute-start(bf16[1,64,18,8]{3,2,1,0:T(8,128)(2,1)S(1)} %get-tuple-element.125), channel_id=1, source_target_pairs={{1,0},{2,1},{3,2},{4,3},{5,4},{6,5},{7,6},{8,7},{9,8},{10,9},{11,1... | collective-permute-start | bytes 55304 | tf_op jit(solution)/shard_map/ppermute | solution.py:21
  71.7 18.2 %collective-permute-done.6 = bf16[1,64,18,8]{3,2,1,0:T(8,128)(2,1)S(1)} collective-permute-done((bf16[1,64,18,8]{3,2,1,0:T(8,128)(2,1)S(1)}, bf16[1,64,18,8]{3,2,1,0:T(8,128)(2,1)S(1)}, u32[]{:S(2)}, u32[]{:S(2)}) %collective-permute-start.6) | collective-permute-done | bytes 18464 | tf_op jit(solution)/shard_map/ppermute | solution.py:18
  92.5 4.1 collective-permute-done.7
  96.6 10.2 %collective-permute-done.2 = bf16[1,64,18,8]{3,2,1,0:T(8,128)(2,1)S(1)} collective-permute-done((bf16[1,64,18,8]{3,2,1,0:T(8,128)(2,1)S(1)}, bf16[1,64,18,8]{3,2,1,0:T(8,128)(2,1)S(1)}, u32[]{:S(2)}, u32[]{:S(2)}) %collective-permute-start.2) | collective-permute-done | bytes 18464 | tf_op jit(solution)/shard_map/ppermute | solution.py:18
  106.7 7.0 %collective-permute-start.11 = (bf16[1,64,18,8]{3,2,1,0:T(8,128)(2,1)}, bf16[1,64,18,8]{3,2,1,0:T(8,128)(2,1)}, u32[]{:S(2)}, u32[]{:S(2)}) collective-permute-start(bf16[1,64,18,8]{3,2,1,0:T(8,128)(2,1)} %get-tuple-element.121), channel_id=1, source_target_pairs={{1,0},{2,1},{3,2},{4,3},{5,4},{6,5},{7,6},{8,7},{9,8},{10,9},{11,1... | collective-permute-start | bytes 55304 | tf_op jit(solution)/shard_map/ppermute | solution.py:21
  216.7 6.1 %all-to-all-start.1 = ((bf16[4,2,16384]{2,1,0:T(2,128)(2,1)}), bf16[4,2,16384]{2,1,0:T(2,128)(2,1)}, u32[]{:S(2)}, u32[]{:S(2)}) async-start(bf16[4,2,16384]{2,1,0:T(2,128)(2,1)} %reshape.268), calls=%async_computation.1 | async-start | bytes 524288 | tf_op jit(solution)/shard_map/all_to_all | solution.py:189
  227.7 5.0 collective-permute-start.28
  254.3 5.1 collective-permute-start.24
  279.1 5.3 collective-permute-start.20
  308.3 65.0 %all-reduce = (f32[64,3,3]{0,2,1:T(4,128)S(1)}, f32[64,64]{1,0:T(8,128)S(1)}, f32[64,64]{1,0:T(8,128)S(1)}) all-reduce(f32[64,3,3]{0,2,1:T(4,128)S(1)} %fusion.173, f32[64,64]{1,0:T(8,128)S(1)} %convolution_add_fusion.9, f32[64,64]{1,0:T(8,128)S(1)} %convolution_add_fusion.6), channel_id=1, replica_groups=mesh['range'=4,'azimuth'=32] {'range','azimuth'}, use_global_device_ids=true, to_apply=%region_38.39 | all-reduce | flops 8768 | bytes 70144 | tf_op jit(solution)/shard_map/psum | solution.py:255
  378.7 4.4 collective-permute-start.16
  388.5 4.8 collective-permute-start.31
  394.7 5.7 %collective-permute-start.27 = (bf16[1,64,18,8]{3,2,1,0:T(8,128)(2,1)S(1)}, bf16[1,64,18,8]{3,2,1,0:T(8,128)(2,1)S(1)}, u32[]{:S(2)}, u32[]{:S(2)}) collective-permute-start(bf16[1,64,18,8]{3,2,1,0:T(8,128)(2,1)S(1)} %get-tuple-element.115), channel_id=1, source_target_pairs={{1,0},{2,1},{3,2},{4,3},{5,4},{6,5},{7,6},{8,7},{9,8},{10,9},{11,1... | collective-permute-start | bytes 55304 | tf_op jit(solution)/shard_map/ppermute | solution.py:21
  401.0 12.4 %collective-permute-done.30 = bf16[1,64,18,8]{3,2,1,0:T(8,128)(2,1)S(1)} collective-permute-done((bf16[1,64,18,8]{3,2,1,0:T(8,128)(2,1)S(1)}, bf16[1,64,18,8]{3,2,1,0:T(8,128)(2,1)S(1)}, u32[]{:S(2)}, u32[]{:S(2)}) %collective-permute-start.30) | collective-permute-done | bytes 18464 | tf_op jit(solution)/shard_map/ppermute | solution.py:18
  413.4 8.7 %collective-permute-start.23 = (bf16[1,64,18,8]{3,2,1,0:T(8,128)(2,1)S(1)}, bf16[1,64,18,8]{3,2,1,0:T(8,128)(2,1)S(1)}, u32[]{:S(2)}, u32[]{:S(2)}) collective-permute-start(bf16[1,64,18,8]{3,2,1,0:T(8,128)(2,1)S(1)} %get-tuple-element.113), channel_id=1, source_target_pairs={{1,0},{2,1},{3,2},{4,3},{5,4},{6,5},{7,6},{8,7},{9,8},{10,9},{11,1... | collective-permute-start | bytes 55304 | tf_op jit(solution)/shard_map/ppermute | solution.py:21
  430.6 4.3 collective-permute-start.19
  434.9 7.5 %collective-permute-done.27 = bf16[1,64,18,8]{3,2,1,0:T(8,128)(2,1)S(1)} collective-permute-done((bf16[1,64,18,8]{3,2,1,0:T(8,128)(2,1)S(1)}, bf16[1,64,18,8]{3,2,1,0:T(8,128)(2,1)S(1)}, u32[]{:S(2)}, u32[]{:S(2)}) %collective-permute-start.27) | collective-permute-done | bytes 18464 | tf_op jit(solution)/shard_map/ppermute | solution.py:21
  462.8 92.5 %all-reduce.4.cloned.1.call-done = (f32[128,128]{1,0:T(8,128)}, f32[128,1024]{1,0:T(8,128)}) async-done(((f32[128,128]{1,0:T(8,128)}, f32[128,1024]{1,0:T(8,128)}), (f32[128,128]{1,0:T(8,128)}, f32[128,1024]{1,0:T(8,128)})) %all-reduce.4.cloned.1.call-update) | async-done | bytes 589840 | tf_op jit(solution)/shard_map/psum | solution.py:255
  (503 shorter events, 244.9 us)
Async XLA Ops:
  10.2 32.3 %all-to-all-start = ((s32[4,1,2]{2,1,0:T(1,128)}), s32[4,1,2]{2,1,0:T(1,128)S(1)}, u32[]{:S(2)}, u32[]{:S(2)}) async-start(s32[4,1,2]{2,1,0:T(1,128)} %bitcast.126), calls=%async_computation | async-start | bytes 4096 | tf_op jit(solution)/shard_map/all_to_all | solution.py:190
  19.0 45.8 %collective-permute-start.12 = (bf16[1,64,1,128]{3,2,1,0:T(2,128)(2,1)S(1)}, bf16[1,64,1,128]{3,2,1,0:T(2,128)(2,1)S(1)}, u32[]{:S(2)}, u32[]{:S(2)}) collective-permute-start(bf16[1,64,1,128]{3,2,1,0:T(2,128)(2,1)S(1)} %get-tuple-element.98), channel_id=1, source_target_pairs={{0,32},{32,64},{64,96},{1,33},{33,65},{65,97},{2,34},{34,66},{66,9... | collective-permute-start | bytes 49160 | tf_op jit(solution)/shard_map/ppermute | solution.py:18
  24.1 33.6 %collective-permute-start.9 = (bf16[1,64,1,128]{3,2,1,0:T(2,128)(2,1)}, bf16[1,64,1,128]{3,2,1,0:T(2,128)(2,1)S(1)}, u32[]{:S(2)}, u32[]{:S(2)}) collective-permute-start(bf16[1,64,1,128]{3,2,1,0:T(2,128)(2,1)} %get-tuple-element.99), channel_id=1, source_target_pairs={{32,0},{64,32},{96,64},{33,1},{65,33},{97,65},{34,2},{66,34},{98,6... | collective-permute-start | bytes 49160 | tf_op jit(solution)/shard_map/ppermute | solution.py:21
  26.1 31.7 %collective-permute-start.8 = (bf16[1,64,1,128]{3,2,1,0:T(2,128)(2,1)S(1)}, bf16[1,64,1,128]{3,2,1,0:T(2,128)(2,1)S(1)}, u32[]{:S(2)}, u32[]{:S(2)}) collective-permute-start(bf16[1,64,1,128]{3,2,1,0:T(2,128)(2,1)S(1)} %get-tuple-element.100), channel_id=1, source_target_pairs={{0,32},{32,64},{64,96},{1,33},{33,65},{65,97},{2,34},{34,66},{66,9... | collective-permute-start | bytes 49160 | tf_op jit(solution)/shard_map/ppermute | solution.py:18
  43.8 124.3 %all-to-all-start.2 = ((bf16[4,2,16384]{2,1,0:T(2,128)(2,1)}), bf16[4,2,16384]{2,1,0:T(2,128)(2,1)}, u32[]{:S(2)}, u32[]{:S(2)}) async-start(bf16[4,2,16384]{2,1,0:T(2,128)(2,1)} %reshape.271), calls=%async_computation.2 | async-start | bytes 524288 | tf_op jit(solution)/shard_map/all_to_all | solution.py:208
  59.1 30.8 %collective-permute-start.6 = (bf16[1,64,18,8]{3,2,1,0:T(8,128)(2,1)S(1)}, bf16[1,64,18,8]{3,2,1,0:T(8,128)(2,1)S(1)}, u32[]{:S(2)}, u32[]{:S(2)}) collective-permute-start(bf16[1,64,18,8]{3,2,1,0:T(8,128)(2,1)S(1)} %get-tuple-element.122), channel_id=1, source_target_pairs={{0,1},{1,2},{2,3},{3,4},{4,5},{5,6},{6,7},{7,8},{8,9},{9,10},{10,1... | collective-permute-start | bytes 55304 | tf_op jit(solution)/shard_map/ppermute | solution.py:18
  59.8 36.8 %collective-permute-start.7 = (bf16[1,64,18,8]{3,2,1,0:T(8,128)(2,1)S(1)}, bf16[1,64,18,8]{3,2,1,0:T(8,128)(2,1)S(1)}, u32[]{:S(2)}, u32[]{:S(2)}) collective-permute-start(bf16[1,64,18,8]{3,2,1,0:T(8,128)(2,1)S(1)} %get-tuple-element.123), channel_id=1, source_target_pairs={{1,0},{2,1},{3,2},{4,3},{5,4},{6,5},{7,6},{8,7},{9,8},{10,9},{11,1... | collective-permute-start | bytes 55304 | tf_op jit(solution)/shard_map/ppermute | solution.py:21
  64.8 42.0 %collective-permute-start.2 = (bf16[1,64,18,8]{3,2,1,0:T(8,128)(2,1)S(1)}, bf16[1,64,18,8]{3,2,1,0:T(8,128)(2,1)S(1)}, u32[]{:S(2)}, u32[]{:S(2)}) collective-permute-start(bf16[1,64,18,8]{3,2,1,0:T(8,128)(2,1)S(1)} %get-tuple-element.124), channel_id=1, source_target_pairs={{0,1},{1,2},{2,3},{3,4},{4,5},{5,6},{6,7},{7,8},{8,9},{9,10},{10,1... | collective-permute-start | bytes 55304 | tf_op jit(solution)/shard_map/ppermute | solution.py:18
  64.8 48.9 %collective-permute-start.3 = (bf16[1,64,18,8]{3,2,1,0:T(8,128)(2,1)S(1)}, bf16[1,64,18,8]{3,2,1,0:T(8,128)(2,1)S(1)}, u32[]{:S(2)}, u32[]{:S(2)}) collective-permute-start(bf16[1,64,18,8]{3,2,1,0:T(8,128)(2,1)S(1)} %get-tuple-element.125), channel_id=1, source_target_pairs={{1,0},{2,1},{3,2},{4,3},{5,4},{6,5},{7,6},{8,7},{9,8},{10,9},{11,1... | collective-permute-start | bytes 55304 | tf_op jit(solution)/shard_map/ppermute | solution.py:21
  71.7 53.6 %collective-permute-start.14 = (bf16[1,64,18,8]{3,2,1,0:T(8,128)(2,1)}, bf16[1,64,18,8]{3,2,1,0:T(8,128)(2,1)}, u32[]{:S(2)}, u32[]{:S(2)}) collective-permute-start(bf16[1,64,18,8]{3,2,1,0:T(8,128)(2,1)} %get-tuple-element.118), channel_id=1, source_target_pairs={{0,1},{1,2},{2,3},{3,4},{4,5},{5,6},{6,7},{7,8},{8,9},{9,10},{10,1... | collective-permute-start | bytes 55304 | tf_op jit(solution)/shard_map/ppermute | solution.py:18
  89.9 35.5 %collective-permute-start.15 = (bf16[1,64,18,8]{3,2,1,0:T(8,128)(2,1)}, bf16[1,64,18,8]{3,2,1,0:T(8,128)(2,1)}, u32[]{:S(2)}, u32[]{:S(2)}) collective-permute-start(bf16[1,64,18,8]{3,2,1,0:T(8,128)(2,1)} %get-tuple-element.119), channel_id=1, source_target_pairs={{1,0},{2,1},{3,2},{4,3},{5,4},{6,5},{7,6},{8,7},{9,8},{10,9},{11,1... | collective-permute-start | bytes 55304 | tf_op jit(solution)/shard_map/ppermute | solution.py:21
  96.6 28.8 %collective-permute-start.10 = (bf16[1,64,18,8]{3,2,1,0:T(8,128)(2,1)}, bf16[1,64,18,8]{3,2,1,0:T(8,128)(2,1)}, u32[]{:S(2)}, u32[]{:S(2)}) collective-permute-start(bf16[1,64,18,8]{3,2,1,0:T(8,128)(2,1)} %get-tuple-element.120), channel_id=1, source_target_pairs={{0,1},{1,2},{2,3},{3,4},{4,5},{5,6},{6,7},{7,8},{8,9},{9,10},{10,1... | collective-permute-start | bytes 55304 | tf_op jit(solution)/shard_map/ppermute | solution.py:18
  216.7 244.0 %all-to-all-start.1 = ((bf16[4,2,16384]{2,1,0:T(2,128)(2,1)}), bf16[4,2,16384]{2,1,0:T(2,128)(2,1)}, u32[]{:S(2)}, u32[]{:S(2)}) async-start(bf16[4,2,16384]{2,1,0:T(2,128)(2,1)} %reshape.268), calls=%async_computation.1 | async-start | bytes 524288 | tf_op jit(solution)/shard_map/all_to_all | solution.py:189
  222.8 332.5 %all-reduce.4.cloned.1.call-start = ((), (), s32[]{:S(2)}) async-start(), calls=%async_computation.3 | async-start | bytes 1179648 | tf_op jit(solution)/shard_map/psum | solution.py:255
  227.7 148.4 %collective-permute-start.28 = (bf16[1,64,1,128]{3,2,1,0:T(2,128)(2,1)}, bf16[1,64,1,128]{3,2,1,0:T(2,128)(2,1)}, u32[]{:S(2)}, u32[]{:S(2)}) collective-permute-start(bf16[1,64,1,128]{3,2,1,0:T(2,128)(2,1)} %get-tuple-element.132), channel_id=1, source_target_pairs={{0,32},{32,64},{64,96},{1,33},{33,65},{65,97},{2,34},{34,66},{66,9... | collective-permute-start | bytes 49160 | tf_op jit(solution)/shard_map/ppermute | solution.py:18
  232.7 146.0 %collective-permute-start.29 = (bf16[1,64,1,128]{3,2,1,0:T(2,128)(2,1)}, bf16[1,64,1,128]{3,2,1,0:T(2,128)(2,1)}, u32[]{:S(2)}, u32[]{:S(2)}) collective-permute-start(bf16[1,64,1,128]{3,2,1,0:T(2,128)(2,1)} %get-tuple-element.133), channel_id=1, source_target_pairs={{32,0},{64,32},{96,64},{33,1},{65,33},{97,65},{34,2},{66,34},{98,6... | collective-permute-start | bytes 49160 | tf_op jit(solution)/shard_map/ppermute | solution.py:21
  254.3 130.1 %collective-permute-start.24 = (bf16[1,64,1,128]{3,2,1,0:T(2,128)(2,1)}, bf16[1,64,1,128]{3,2,1,0:T(2,128)(2,1)}, u32[]{:S(2)}, u32[]{:S(2)}) collective-permute-start(bf16[1,64,1,128]{3,2,1,0:T(2,128)(2,1)} %get-tuple-element.130), channel_id=1, source_target_pairs={{0,32},{32,64},{64,96},{1,33},{33,65},{65,97},{2,34},{34,66},{66,9... | collective-permute-start | bytes 49160 | tf_op jit(solution)/shard_map/ppermute | solution.py:18
  259.4 126.9 %collective-permute-start.25 = (bf16[1,64,1,128]{3,2,1,0:T(2,128)(2,1)}, bf16[1,64,1,128]{3,2,1,0:T(2,128)(2,1)}, u32[]{:S(2)}, u32[]{:S(2)}) collective-permute-start(bf16[1,64,1,128]{3,2,1,0:T(2,128)(2,1)} %get-tuple-element.131), channel_id=1, source_target_pairs={{32,0},{64,32},{96,64},{33,1},{65,33},{97,65},{34,2},{66,34},{98,6... | collective-permute-start | bytes 49160 | tf_op jit(solution)/shard_map/ppermute | solution.py:21
  279.1 109.4 %collective-permute-start.20 = (bf16[1,64,1,128]{3,2,1,0:T(2,128)(2,1)}, bf16[1,64,1,128]{3,2,1,0:T(2,128)(2,1)}, u32[]{:S(2)}, u32[]{:S(2)}) collective-permute-start(bf16[1,64,1,128]{3,2,1,0:T(2,128)(2,1)} %get-tuple-element.128), channel_id=1, source_target_pairs={{0,32},{32,64},{64,96},{1,33},{33,65},{65,97},{2,34},{34,66},{66,9... | collective-permute-start | bytes 49160 | tf_op jit(solution)/shard_map/ppermute | solution.py:18
  388.5 37.0 %collective-permute-start.31 = (bf16[1,64,18,8]{3,2,1,0:T(8,128)(2,1)S(1)}, bf16[1,64,18,8]{3,2,1,0:T(8,128)(2,1)S(1)}, u32[]{:S(2)}, u32[]{:S(2)}) collective-permute-start(bf16[1,64,18,8]{3,2,1,0:T(8,128)(2,1)S(1)} %get-tuple-element.117), channel_id=1, source_target_pairs={{1,0},{2,1},{3,2},{4,3},{5,4},{6,5},{7,6},{8,7},{9,8},{10,9},{11,1... | collective-permute-start | bytes 55304 | tf_op jit(solution)/shard_map/ppermute | solution.py:21
  393.3 37.3 %collective-permute-start.26 = (bf16[1,64,18,8]{3,2,1,0:T(8,128)(2,1)S(1)}, bf16[1,64,18,8]{3,2,1,0:T(8,128)(2,1)S(1)}, u32[]{:S(2)}, u32[]{:S(2)}) collective-permute-start(bf16[1,64,18,8]{3,2,1,0:T(8,128)(2,1)S(1)} %get-tuple-element.114), channel_id=1, source_target_pairs={{0,1},{1,2},{2,3},{3,4},{4,5},{5,6},{6,7},{7,8},{8,9},{9,10},{10,1... | collective-permute-start | bytes 55304 | tf_op jit(solution)/shard_map/ppermute | solution.py:18
  394.7 47.7 %collective-permute-start.27 = (bf16[1,64,18,8]{3,2,1,0:T(8,128)(2,1)S(1)}, bf16[1,64,18,8]{3,2,1,0:T(8,128)(2,1)S(1)}, u32[]{:S(2)}, u32[]{:S(2)}) collective-permute-start(bf16[1,64,18,8]{3,2,1,0:T(8,128)(2,1)S(1)} %get-tuple-element.115), channel_id=1, source_target_pairs={{1,0},{2,1},{3,2},{4,3},{5,4},{6,5},{7,6},{8,7},{9,8},{10,9},{11,1... | collective-permute-start | bytes 55304 | tf_op jit(solution)/shard_map/ppermute | solution.py:21
  400.5 47.0 %collective-permute-start.22 = (bf16[1,64,18,8]{3,2,1,0:T(8,128)(2,1)S(1)}, bf16[1,64,18,8]{3,2,1,0:T(8,128)(2,1)S(1)}, u32[]{:S(2)}, u32[]{:S(2)}) collective-permute-start(bf16[1,64,18,8]{3,2,1,0:T(8,128)(2,1)S(1)} %get-tuple-element.112), channel_id=1, source_target_pairs={{0,1},{1,2},{2,3},{3,4},{4,5},{5,6},{6,7},{7,8},{8,9},{9,10},{10,1... | collective-permute-start | bytes 55304 | tf_op jit(solution)/shard_map/ppermute | solution.py:18
  413.4 37.7 %collective-permute-start.23 = (bf16[1,64,18,8]{3,2,1,0:T(8,128)(2,1)S(1)}, bf16[1,64,18,8]{3,2,1,0:T(8,128)(2,1)S(1)}, u32[]{:S(2)}, u32[]{:S(2)}) collective-permute-start(bf16[1,64,18,8]{3,2,1,0:T(8,128)(2,1)S(1)} %get-tuple-element.113), channel_id=1, source_target_pairs={{1,0},{2,1},{3,2},{4,3},{5,4},{6,5},{7,6},{8,7},{9,8},{10,9},{11,1... | collective-permute-start | bytes 55304 | tf_op jit(solution)/shard_map/ppermute | solution.py:21
  (144 other events, 2322.4 us)
Sparse Core Ops, SparseCore 0:
  376.2 179.0 all-reduce.3
where the time goes:
time: 575 us; the launch traced here: 566 us
  waiting for transfers between devices  161 us (28%)
  starting transfers between devices  119 us (21%)
  local copies, waits for them, and re-layouts  94.2 us (16%)
  blocking collectives  65 us (11%)
  matrix products  62.9 us (11%)
  other arithmetic  46.4 us (8%)
  between operations  16.7 us (3%)
    psum x1, waiting for transfers between devices, on_device(): lax.psum((grad_kernel, grad_gate, grad_cand, grad_recur, grad_down), ('ra...  92.5 us
    psum x1, blocking collectives, on_device(): lax.psum((grad_kernel, grad_gate, grad_cand, grad_recur, grad_down), ('ra...  65 us
    ppermute x16, starting transfers between devices, extended(): lax.ppermute(lax.slice_in_dim(block, 0, width, axis=dim), axis, backward)  60 us
    ppermute x16, waiting for transfers between devices, extended(): lax.ppermute(lax.slice_in_dim(block, block.shape[dim] - width, None, axis...  45 us
    ppermute x16, starting transfers between devices, extended(): lax.ppermute(lax.slice_in_dim(block, block.shape[dim] - width, None, axis...  42.5 us
    dot_general x18, matrix products, back_product(): lax.dot_general(weight, grads, (((0,), (0,)), ((), ())), preferred_elemen...  24.8 us
    ppermute x16, waiting for transfers between devices, extended(): lax.ppermute(lax.slice_in_dim(block, 0, width, axis=dim), axis, backward)  23.9 us
    dot_general x16, matrix products, cross_cells(): lax.dot_general(left, right, (((1,), (1,)), ((), ())), preferred_element_...  16.9 us
  transfers between devices with their start and end apart: 36, of which 12 were waited for; matrix products, arithmetic and copies ran while one was open for 26% of the time, Pallas kernels for 0%

commit v1 on v0

v1 whole, which is shorter than its diff:
```python
import functools
import math

import jax
import jax.numpy as jnp
from jax import lax
from jax.experimental import pallas as pl
from jax.experimental.pallas import tpu as pltpu
from jax.sharding import PartitionSpec as P

MESH = pl.DeviceIdType.MESH
F32 = jnp.float32
BF16 = jnp.bfloat16
I32 = jnp.int32

CH = 64
NT = 4
NROW = 16
NCOL = 128
CELLS = NROW * NCOL
NAT = CH * NROW
CO = 128
SPAN = 512
GROUP = 16


def iota(shape, dim):
    return lax.broadcasted_iota(I32, shape, dim)


def nn(left, right):
    return lax.dot_general(left, right, (((1,), (0,)), ((), ())), preferred_element_type=F32)


def nt(left, right):
    return lax.dot_general(left, right, (((1,), (1,)), ((), ())), preferred_element_type=F32)


def remote(src, dst, send_sem, recv_sem, device):
    return pltpu.make_async_remote_copy(
        src_ref=src,
        dst_ref=dst,
        send_sem=send_sem,
        recv_sem=recv_sem,
        device_id=device,
        device_id_type=MESH,
    )


def kernel(
    nr,
    na,
    scale,
    feat,
    state,
    kern,
    gate,
    cand,
    recur,
    down,
    owner,
    dest,
    cot,
    cart,
    gfeat,
    gstate,
    gkern,
    ggate,
    gcand,
    grecur,
    gdown,
    fx,
    xs,
    stk,
    hs,
    s_a,
    s_b,
    s_c,
    s_r,
    s_u,
    flow_in,
    pt,
    hcat,
    perm,
    pick,
    spread,
    wall,
    wall_t,
    wp,
    wb,
    wk,
    dlt,
    dcv,
    carry,
    dwacc,
    gkacc,
    gd,
    coracc,
    row_s,
    row_r,
    col_s,
    col_r,
    cor_s,
    cor_r,
    cot_all,
    key_all,
    blk_all,
    gds,
    gdr,
    gd2,
    gd2r,
    gd3,
    sm1s,
    sm1r,
    sm2,
    sm2r,
    sm3,
    halo_ss,
    halo_rs,
    cot_ss,
    cot_rs,
    key_ss,
    key_rs,
    blk_ss,
    blk_rs,
    xy_ss,
    xy_rs,
    z_ss,
    z_rs,
):
    r = lax.axis_index("range")
    a = lax.axis_index("azimuth")
    n2 = na // 2
    n1 = nr * 2
    k2 = a // 2
    zl = a % 2
    k1 = r * 2 + zl

    def ring_r(d):
        return lax.rem(r + d + nr, nr)

    def ring_a(d):
        return lax.rem(a + d + na, na)

    def xy_device(d):
        return (r, lax.rem(k2 + d, n2) * 2 + zl)

    def z_device(d):
        m = lax.rem(k1 + d, n1)
        return (m // 2, k2 * 2 + m % 2)

    barrier = pltpu.get_barrier_semaphore()

    def greet(device):
        pl.semaphore_signal(barrier, inc=1, device_id=device, device_id_type=MESH)

    diagonals = [(-1, -1), (-1, 1), (1, -1), (1, 1)]
    for da in (-1, 1):
        greet((r, ring_a(da)))
    for dr, da in diagonals:
        greet((ring_r(dr), ring_a(da)))

    def greet_xy(d, c):
        greet(xy_device(d))
        return c

    def greet_z(d, c):
        greet(z_device(d))
        return c

    lax.fori_loop(1, n2, greet_xy, 0)
    lax.fori_loop(1, n1, greet_z, 0)

    lane = iota((GROUP, NCOL), 1)
    lane8 = lane // 8
    lane16 = lane // 16

    def chans(g):
        return pl.ds(pl.multiple_of(g * GROUP, GROUP), GROUP)

    def feature_row(t, g, i):
        return fx[pl.ds(t * NAT + g * GROUP * NROW + i, GROUP, stride=NROW), :]

    def dconv_row(t, g, i):
        return dcv[t, chans(g), pl.ds(i * NCOL, NCOL)]

    def pack(ph, row):
        def step(n, c):
            t, g = n // 4, n % 4
            cs = chans(g)
            left = jnp.zeros((GROUP, NCOL), F32)
            right = jnp.zeros((GROUP, NCOL), F32)
            for i in range(NROW):
                x = row(t, g, i)
                y = pltpu.roll(x, (8 * i + 8) % NCOL, 1)
                right = jnp.where(lane8 == i, y, right)
                left = jnp.where(lane8 == (i + 1) % 16, y, left)
                if i in (0, NROW - 1):
                    end = 0 if i == 0 else 1
                    row_s[ph, end, t, cs, :] = x.astype(BF16)
                    spot = 2 * t + end
                    y = pltpu.roll(x, (16 * spot + 8) % NCOL, 1)
                    coracc[cs, :] = jnp.where(lane16 == spot, y, coracc[cs, :])
            col_s[ph, 0, t, cs, :] = pltpu.roll(left, NCOL - 16, 1).astype(BF16)
            col_s[ph, 1, t, cs, :] = right.astype(BF16)
            return c

        lax.fori_loop(0, 4 * NT, step, 0)
        cor_s[ph] = coracc[...].astype(BF16)

    def halo_copies(ph):
        copies = []
        for end, d in ((0, -1), (1, 1)):
            n = len(copies)
            copies.append(
                remote(
                    row_s.at[ph, end],
                    row_r.at[ph, 1 - end],
                    halo_ss.at[ph, n],
                    halo_rs.at[ph, n],
                    (ring_r(d), a),
                )
            )
        for end, d in ((0, -1), (1, 1)):
            n = len(copies)
            copies.append(
                remote(
                    col_s.at[ph, end],
                    col_r.at[ph, 1 - end],
                    halo_ss.at[ph, n],
                    halo_rs.at[ph, n],
                    (r, ring_a(d)),
                )
            )
        for j, (dr, da) in enumerate(diagonals):
            n = len(copies)
            copies.append(
                remote(
                    cor_s.at[ph],
                    cor_r.at[ph, 3 - j],
                    halo_ss.at[ph, n],
                    halo_rs.at[ph, n],
                    (ring_r(dr), ring_a(da)),
                )
            )
        return copies

    has_low = (r > 0).astype(F32)
    has_high = (r < nr - 1).astype(F32)

    def windows(ph, row, t, g):
        cs = chans(g)
        halo_l = col_r[ph, 0, t, cs, :].astype(F32)
        halo_h = col_r[ph, 1, t, cs, :].astype(F32)
        out = [[None] * (NROW + 2) for _ in range(3)]

        def put(pos, x, low, high):
            out[0][pos] = jnp.where(lane < 8, low, pltpu.roll(x, 8, 1))
            out[1][pos] = x
            out[2][pos] = jnp.where(lane >= NCOL - 8, high, pltpu.roll(x, NCOL - 8, 1))

        for i in range(NROW):
            x = row(t, g, i)
            w = pltpu.roll(jnp.where(lane8 == i, halo_l, halo_h), (NCOL - 8 * i) % NCOL, 1)
            put(i + 1, x, w, w)
        for end in (0, 1):
            keep = has_low if end == 0 else has_high
            spot = 2 * t + (1 - end)
            x = row_r[ph, end, t, cs, :].astype(F32) * keep
            c_l = cor_r[ph, 2 * end, cs, :].astype(F32) * keep
            c_h = cor_r[ph, 2 * end + 1, cs, :].astype(F32) * keep
            low = pltpu.roll(c_l, lax.rem(NCOL - 16 * spot, NCOL), 1)
            high = pltpu.roll(c_h, 112 - 16 * spot, 1)
            put(0 if end == 0 else NROW + 1, x, low, high)
        return out

    def convolve(shifted, g, flipped, store):
        cs = chans(g)
        taps = [wk[8 - n if flipped else n, cs, :] for n in range(9)]
        for i in range(NROW):
            total = taps[0] * shifted[0][i]
            for n in range(1, 9):
                total = total + taps[n] * shifted[n % 3][i + n // 3]
            store(i, total)

    def widen(n, c):
        at = pl.ds(pl.multiple_of(n * 256, 256), 256)
        fx[at, :] = feat[at, :].astype(F32)
        return c

    lax.fori_loop(0, NT * NAT // 256, widen, 0)
    coracc[...] = jnp.zeros((CH, NCOL), F32)
    pack(0, feature_row)
    key_row = iota((8, NCOL), 0)
    keys = jnp.zeros((8, NCOL), I32)
    for b in range(NT):
        keys = jnp.where(key_row == b, owner[0, 0, b] * NT + dest[0, 0, b], keys)
    key_all[r] = keys

    pl.semaphore_wait(barrier, 6 + (n2 - 1) + (n1 - 1))

    halo0 = halo_copies(0)
    for copy in halo0:
        copy.start()
    cot_copies = []
    key_copies = []
    for d in range(1, nr):
        device = (ring_r(d), a)
        key_copies.append(
            remote(key_all.at[r], key_all.at[r], key_ss.at[d - 1], key_rs.at[d - 1], device)
        )
        cot_copies.append(remote(cot, cot_all.at[r], cot_ss.at[d - 1], cot_rs.at[d - 1], device))
    for copy in cot_copies + key_copies:
        copy.start()

    cot_all[r] = cot[...]

    def make_perm(n, c):
        at = pl.multiple_of(n * 128, 128)
        src = iota((128, 1), 0) + at
        to = (src % 4) * 256 + ((src // 4) % 4) * CH + src // 16
        perm[pl.ds(at, 128), :] = (iota((128, 1024), 1) == to).astype(F32).astype(BF16)
        return c

    lax.fori_loop(0, 8, make_perm, 0)

    def make_pick(n, c):
        at = pl.multiple_of(n * 128, 128)
        src = iota((128, 1), 0) + at
        to = (src % 4) * 128 + (src // 128) * 32 + (src % 128) // 4
        pick[pl.ds(at, 128), :] = (iota((128, SPAN), 1) == to).astype(F32).astype(BF16)
        return c

    lax.fori_loop(0, 4, make_pick, 0)
    dst = iota((128, SPAN), 1)
    spread[...] = (iota((128, SPAN), 0) == (dst // 128) * 32 + (dst % 128) // 4).astype(F32).astype(BF16)

    place = iota((CH, 2 * CH), 1) - iota((CH, 2 * CH), 0)
    wall[0 : 2 * CH, :] = gate[...]
    wall[2 * CH : 3 * CH, :] = nn(cand[...], (place == 0).astype(F32).astype(BF16)).astype(BF16)
    wall[3 * CH : 4 * CH, :] = nn(recur[...], (place == CH).astype(F32).astype(BF16)).astype(BF16)
    wall_t[...] = wall[...].astype(F32).T.astype(BF16)
    for q in range(4):
        part = nn(down[...], perm[:, q * 256 : (q + 1) * 256])
        wp[:, q * 256 : (q + 1) * 256] = part.astype(BF16)
        wb[:, q * 128 : (q + 1) * 128] = part.T.astype(BF16)
    for n in range(9):
        line = kern[n // 3, n % 3 : n % 3 + 1, :]
        wk[n] = jnp.broadcast_to(line, (NCOL, CH)).T
    gstate[...] = state[...].astype(F32)
    for i in range(NROW):
        hs[0, :, i * NCOL : (i + 1) * NCOL] = gstate[pl.ds(i, CH, stride=NROW), :]

    for copy in halo0:
        copy.wait_recv()

    def conv_forward(n, c):
        t, g = n // 4, n % 4
        cs = chans(g)
        shifted = windows(0, feature_row, t, g)
        for b in range(3):
            for i in range(NROW + 2):
                xs[t, b, i, cs, :] = shifted[b][i]

        def store(i, total):
            stk[t, cs, i * NCOL : (i + 1) * NCOL] = total.astype(BF16)

        convolve(shifted, g, False, store)
        return c

    lax.fori_loop(0, 4 * NT, conv_forward, 0)

    def forward(t, c):
        for ic in range(4):
            ls = slice(ic * SPAN, (ic + 1) * SPAN)
            h = hs[t, :, ls]
            stk[t, CH : 2 * CH, ls] = h.astype(BF16)
            pre = nn(wall[...], stk[t, :, ls])
            u = 0.5 * jnp.tanh(0.5 * pre[0:CH]) + 0.5
            z = 0.5 * jnp.tanh(0.5 * pre[CH : 2 * CH]) + 0.5
            rec = pre[3 * CH : 4 * CH]
            act = jnp.tanh(pre[2 * CH : 3 * CH] + z * rec)
            gap = act - h
            step = u * gap
            new = h + step
            hs[t + 1, :, ls] = new
            s_u[t, :, ls] = u
            s_r[t, :, ls] = z
            s_a[t, :, ls] = step * (1.0 - u)
            s_b[t, :, ls] = u * (1.0 - act * act)
            s_c[t, :, ls] = rec * z * (1.0 - z)
            new_bf = new.astype(BF16)
            for p in range(4):
                hcat[p * CH : (p + 1) * CH, ic * NCOL : (ic + 1) * NCOL] = new_bf[
                    :, p * NCOL : (p + 1) * NCOL
                ]
        sorted_lanes = nn(hcat[...], pick[...])
        for q in range(4):
            pt[t, q * 256 : (q + 1) * 256, :] = sorted_lanes[:, q * 128 : (q + 1) * 128].astype(BF16)
        blk_all[r, t] = nn(wp[...], pt[t]).astype(BF16)
        return c

    for t in range(NT):
        forward(t, 0)

    blk_copies = []
    for d in range(1, nr):
        device = (ring_r(d), a)
        blk_copies.append(
            remote(blk_all.at[r], blk_all.at[r], blk_ss.at[d - 1], blk_rs.at[d - 1], device)
        )
    for copy in blk_copies:
        copy.start()

    for copy in cot_copies:
        copy.wait_recv()
    gd[...] = jnp.zeros(gd.shape, F32)
    sub = iota((CO, SPAN), 1) % 4

    def coarse_back(t, c):
        block = cot_all[owner[0, 0, t], dest[0, 0, t]]
        wide = nn(block, spread[...])
        each = [jnp.where(sub == q, wide, 0.0).astype(BF16) for q in range(4)]
        flow_in[t] = nn(wb[...], jnp.concatenate(each, axis=0))
        gd[...] += nt(block, pt[t])
        return c

    for t in range(NT):
        coarse_back(t, 0)

    fold_rows, fold_cols = gds.shape[1], gds.shape[2]
    own_rows = CO // n2
    parts = fold_rows // own_rows
    natural = nt(gd[...].astype(BF16), perm[...])
    for k in range(n2):
        mine = natural[k * own_rows : (k + 1) * own_rows]
        gds[k] = jnp.concatenate(
            [mine[:, j * fold_cols : (j + 1) * fold_cols] for j in range(parts)], axis=0
        ).astype(BF16)

    def start_all(count, make):
        def go(d, c):
            make(d).start()
            return c

        lax.fori_loop(1, count, go, 0)

    def wait_all(count, make):
        def go(d, c):
            make(d).wait_recv()
            return c

        lax.fori_loop(1, count, go, 0)

    def sent_all(count, make):
        def go(d, c):
            make(d).wait_send()
            return c

        lax.fori_loop(1, count, go, 0)

    def scatter_copy(slot, src, dst):
        def make(d):
            to = lax.rem(k2 + d, n2)
            return remote(
                src(to), dst.at[d - 1], xy_ss.at[slot, d - 1], xy_rs.at[slot, d - 1], xy_device(d)
            )

        return make

    def z_copy(slot, src, dst):
        def make(d):
            return remote(src, dst.at[d - 1], z_ss.at[slot, d - 1], z_rs.at[slot, d - 1], z_device(d))

        return make

    def gather_copy(slot, buf):
        def make(d):
            return remote(
                buf.at[k2], buf.at[k2], xy_ss.at[slot, d - 1], xy_rs.at[slot, d - 1], xy_device(d)
            )

        return make

    big1 = scatter_copy(0, lambda to: gds.at[to], gdr)
    big2 = z_copy(0, gd2, gd2r)
    big3 = gather_copy(1, gd3)
    sm_rows = 4 * CH // n2
    small1 = scatter_copy(
        2, lambda to: sm1s.at[pl.ds(pl.multiple_of(to * sm_rows, sm_rows), sm_rows)], sm1r
    )
    small2 = z_copy(1, sm2, sm2r)
    small3 = gather_copy(3, sm3)

    def sum_slots(own, buf, count):
        def add(d, total):
            return total + buf[d].astype(F32)

        return lax.fori_loop(0, count, add, own)

    start_all(n2, big1)

    def big_second():
        wait_all(n2, big1)
        gd2[...] = sum_slots(gds[k2].astype(F32), gdr, n2 - 1)
        start_all(n1, big2)

    def big_third():
        wait_all(n1, big2)
        total = sum_slots(gd2[...], gd2r, n1 - 1) * scale
        gd3[k2] = jnp.concatenate(
            [total[j * own_rows : (j + 1) * own_rows] for j in range(parts)], axis=1
        )
        start_all(n2, big3)

    carry[...] = jnp.zeros(carry.shape, F32)
    dwacc[...] = jnp.zeros(dwacc.shape, F32)
    gkacc[...] = jnp.zeros(gkacc.shape, F32)

    def backward(n, c):
        t = NT - 1 - n
        for ic in range(4):
            ls = slice(ic * SPAN, (ic + 1) * SPAN)
            rows_in = [
                flow_in[t, p * CH : (p + 1) * CH, ic * NCOL : (ic + 1) * NCOL] for p in range(4)
            ]
            flow = carry[:, ls] + jnp.concatenate(rows_in, axis=1)
            act = flow * s_b[t, :, ls]
            dlt[0:CH, ls] = (flow * s_a[t, :, ls]).astype(BF16)
            dlt[CH : 2 * CH, ls] = (act * s_c[t, :, ls]).astype(BF16)
            dlt[2 * CH : 3 * CH, ls] = act.astype(BF16)
            dlt[3 * CH : 4 * CH, ls] = (act * s_r[t, :, ls]).astype(BF16)
            rev = nn(wall_t[...], dlt[:, ls])
            dcv[t, :, ls] = rev[0:CH].astype(BF16).astype(F32)
            carry[:, ls] = (1.0 - s_u[t, :, ls]) * flow + rev[CH : 2 * CH]
        dwacc[...] += nt(dlt[...], stk[t])

        def kernel_grad(g, c2):
            cs = chans(g)
            grads = [dcv[t, cs, i * NCOL : (i + 1) * NCOL] for i in range(NROW)]
            for tap in range(9):
                total = gkacc[tap, cs, :]
                for i in range(NROW):
                    total = total + grads[i] * xs[t, tap % 3, i + tap // 3, cs, :]
                gkacc[tap, cs, :] = total
            return c2

        lax.fori_loop(0, 4, kernel_grad, 0)
        pl.when(n == 1)(big_second)
        pl.when(n == 3)(big_third)
        return c

    lax.fori_loop(0, NT, backward, 0)

    lanes = iota((CH, NCOL), 1)
    sm1s[0 : 2 * CH, :] = dwacc[0 : 2 * CH, :]
    sm1s[2 * CH : 3 * CH, :] = jnp.where(
        lanes < CH, dwacc[2 * CH : 3 * CH, :], dwacc[3 * CH : 4 * CH, :]
    )
    columns = jnp.zeros((CH, NCOL), F32)
    for tap in range(9):
        columns = jnp.where(lanes == tap, jnp.sum(gkacc[tap], axis=1, keepdims=True), columns)
    sm1s[3 * CH : 4 * CH, :] = columns
    start_all(n2, small1)

    coracc[...] = jnp.zeros((CH, NCOL), F32)
    pack(1, dconv_row)
    halo1 = halo_copies(1)
    for copy in halo1:
        copy.start()

    for i in range(NROW):
        gstate[pl.ds(i, CH, stride=NROW), :] = carry[:, i * NCOL : (i + 1) * NCOL]

    wait_all(n2, small1)
    own = sm1s[pl.ds(pl.multiple_of(k2 * sm_rows, sm_rows), sm_rows), :]
    sm2[...] = sum_slots(own, sm1r, n2 - 1)
    start_all(n1, small2)

    for copy in key_copies + blk_copies:
        copy.wait_recv()

    def gather_blocks(n, c):
        at = pl.ds(pl.multiple_of(n * 32, 32), 32)
        totals = [jnp.zeros((32, NCOL), F32) for _ in range(NT)]
        for src in range(nr):
            for b in range(NT):
                key = key_all[src, b : b + 1, :]
                block = blk_all[src, b, at, :].astype(F32)
                for d in range(NT):
                    totals[d] = totals[d] + jnp.where(key == r * NT + d, block, 0.0)
        for d in range(NT):
            cart[d, at, :] = totals[d]
        return c

    lax.fori_loop(0, 4, gather_blocks, 0)

    wait_all(n1, small2)
    sm3[k2] = sum_slots(sm2[...], sm2r, n1 - 1) * scale
    start_all(n2, small3)

    for copy in halo1:
        copy.wait_recv()

    def conv_backward(n, c):
        t, g = n // 4, n % 4
        shifted = windows(1, dconv_row, t, g)

        def store(i, total):
            fx[pl.ds(t * NAT + g * GROUP * NROW + i, GROUP, stride=NROW), :] = total

        convolve(shifted, g, True, store)
        at = pl.ds(pl.multiple_of(n * 256, 256), 256)
        gfeat[at, :] = fx[at, :].astype(BF16)
        return c

    lax.fori_loop(0, 4 * NT, conv_backward, 0)

    wait_all(n2, big3)
    gdown[...] = gd3[...].reshape(CO, 16 * CH)

    wait_all(n2, small3)
    small = sm3[...].reshape(4 * CH, NCOL)
    ggate[...] = small[0 : 2 * CH]
    middle = small[2 * CH : 3 * CH]
    gcand[...] = middle[:, 0:CH]
    grecur[...] = pltpu.roll(middle, CH, 1)[:, 0:CH]
    lines = small[3 * CH : 4 * CH].T
    for tap in range(9):
        gkern[tap // 3, tap % 3 : tap % 3 + 1, :] = lines[tap : tap + 1, :]

    for copy in halo0 + halo1 + cot_copies + key_copies + blk_copies:
        copy.wait_send()
    sent_all(n2, big1)
    sent_all(n1, big2)
    sent_all(n2, big3)
    sent_all(n2, small1)
    sent_all(n1, small2)
    sent_all(n2, small3)


def on_device(nr, na, *args):
    (features, state_init, kern, gate, cand, recur, down, owner_map, dest_map, cart_cot) = args
    scale = 1.0 / math.sqrt(NT * CELLS * nr * na)
    n2, n1 = na // 2, nr * 2
    own_rows = CO // n2
    parts = max(1, 16 // own_rows)
    fold = (own_rows * parts, 16 * CH // parts)
    sm_rows = 4 * CH // n2
    vmem = pl.BlockSpec(memory_space=pltpu.VMEM)
    smem = pl.BlockSpec(memory_space=pltpu.SMEM)
    dma = pltpu.SemaphoreType.DMA
    cells = (NT, CH, CELLS)
    scratch = [
        pltpu.VMEM((NT * NAT, NCOL), F32),
        pltpu.VMEM((NT, 3, NROW + 2, CH, NCOL), F32),
        pltpu.VMEM((NT, 2 * CH, CELLS), BF16),
        pltpu.VMEM((NT + 1, CH, CELLS), F32),
        pltpu.VMEM(cells, F32),
        pltpu.VMEM(cells, F32),
        pltpu.VMEM(cells, F32),
        pltpu.VMEM(cells, F32),
        pltpu.VMEM(cells, F32),
        pltpu.VMEM((NT, 4 * CH, SPAN), F32),
        pltpu.VMEM((NT, 16 * CH, 128), BF16),
        pltpu.VMEM((4 * CH, SPAN), BF16),
        pltpu.VMEM((1024, 1024), BF16),
        pltpu.VMEM((SPAN, SPAN), BF16),
        pltpu.VMEM((128, SPAN), BF16),
        pltpu.VMEM((4 * CH, 2 * CH), BF16),
        pltpu.VMEM((2 * CH, 4 * CH), BF16),
        pltpu.VMEM((CO, 16 * CH), BF16),
        pltpu.VMEM((4 * CH, 4 * CO), BF16),
        pltpu.VMEM((9, CH, NCOL), F32),
        pltpu.VMEM((4 * CH, CELLS), BF16),
        pltpu.VMEM(cells, F32),
        pltpu.VMEM((CH, CELLS), F32),
        pltpu.VMEM((4 * CH, 2 * CH), F32),
        pltpu.VMEM((9, CH, NCOL), F32),
        pltpu.VMEM((CO, 16 * CH), F32),
        pltpu.VMEM((CH, NCOL), F32),
        pltpu.VMEM((2, 2, NT, CH, NCOL), BF16),
        pltpu.VMEM((2, 2, NT, CH, NCOL), BF16),
        pltpu.VMEM((2, 2, NT, CH, NCOL), BF16),
        pltpu.VMEM((2, 2, NT, CH, NCOL), BF16),
        pltpu.VMEM((2, CH, NCOL), BF16),
        pltpu.VMEM((2, 4, CH, NCOL), BF16),
        pltpu.VMEM((nr, NT, CO, 128), BF16),
        pltpu.VMEM((nr, 8, 128), I32),
        pltpu.VMEM((nr, NT, CO, 128), BF16),
        pltpu.VMEM((n2, *fold), BF16),
        pltpu.VMEM((n2 - 1, *fold), BF16),
        pltpu.VMEM(fold, F32),
        pltpu.VMEM((n1 - 1, *fold), F32),
        pltpu.VMEM((n2, own_rows, 16 * CH), F32),
        pltpu.VMEM((4 * CH, NCOL), F32),
        pltpu.VMEM((n2 - 1, sm_rows, NCOL), F32),
        pltpu.VMEM((sm_rows, NCOL), F32),
        pltpu.VMEM((n1 - 1, sm_rows, NCOL), F32),
        pltpu.VMEM((n2, sm_rows, NCOL), F32),
        dma((2, 8)),
        dma((2, 8)),
        dma((nr - 1,)),
        dma((nr - 1,)),
        dma((nr - 1,)),
        dma((nr - 1,)),
        dma((nr - 1,)),
        dma((nr - 1,)),
        dma((4, n2 - 1)),
        dma((4, n2 - 1)),
        dma((2, n1 - 1)),
        dma((2, n1 - 1)),
    ]
    out = pl.pallas_call(
        functools.partial(kernel, nr, na, scale),
        out_shape=(
            jax.ShapeDtypeStruct((NT, CO, 128), F32),
            jax.ShapeDtypeStruct((NT * NAT, NCOL), BF16),
            jax.ShapeDtypeStruct((NAT, NCOL), F32),
            jax.ShapeDtypeStruct((3, 3, CH), F32),
            jax.ShapeDtypeStruct((2 * CH, 2 * CH), F32),
            jax.ShapeDtypeStruct((CH, CH), F32),
            jax.ShapeDtypeStruct((CH, CH), F32),
            jax.ShapeDtypeStruct((CO, 16 * CH), F32),
        ),
        in_specs=[vmem] * 7 + [smem] * 2 + [vmem],
        out_specs=(vmem,) * 8,
        scratch_shapes=scratch,
        compiler_params=pltpu.CompilerParams(
            collective_id=0, has_side_effects=True, vmem_limit_bytes=60 * 1024 * 1024
        ),
        name="section",
    )(
        features.reshape(NT * NAT, NCOL),
        state_init.reshape(NAT, NCOL),
        kern.transpose(1, 2, 0),
        gate,
        cand,
        recur,
        down,
        owner_map,
        dest_map,
        cart_cot.reshape(NT, CO, 128),
    )
    cart, gfeat, gstate, gkern, ggate, gcand, grecur, gdown = out
    return (
        cart.reshape(1, 1, NT, CO, 128),
        gfeat.reshape(NT, CH, NROW, NCOL),
        gstate.reshape(CH, NROW, NCOL),
        gkern.transpose(2, 0, 1),
        ggate,
        gcand,
        grecur,
        gdown,
    )


def solution(mesh):
    nr, na = mesh.shape["range"], mesh.shape["azimuth"]
    tile = P(None, "range", "azimuth")
    maps = P("range", "azimuth", None)
    cartesian = P("range", "azimuth", None, None, None)
    features = P(None, None, "range", "azimuth")
    return jax.shard_map(
        functools.partial(on_device, nr, na),
        mesh=mesh,
        in_specs=(features, tile, P(), P(), P(), P(), P(), maps, maps, cartesian),
        out_specs=(cartesian, features, tile, P(), P(), P(), P(), P()),
        check_vma=False,
    )
```

time: 575 us -> 70.2 us (0.12); the launches traced: 566 us -> 69.9 us
  waiting for transfers between devices: 161 us -> 0 us
  starting transfers between devices: 119 us -> 0 us
  local copies, waits for them, and re-layouts: 94.2 us -> 8.44 us
  blocking collectives: 65 us -> 0 us
  matrix products: 62.9 us -> 0 us
  Pallas kernels: 0 us -> 60.8 us
  other arithmetic: 46.4 us -> 0 us
  between operations: 16.7 us -> 0.66 us
    ppermute x32 -> x0, starting transfers between devices: 102 us -> none  [the longest x16 60 us: extended(): lax.ppermute(lax.slice_in_dim(block, 0, width, axis=dim), axis, backward)]
    psum x1 -> x0, waiting for transfers between devices: 92.5 us -> none  [on_device(): lax.psum((grad_kernel, grad_gate, grad_cand, grad_recur, grad_down), ('ra...]
    ppermute x32 -> x0, waiting for transfers between devices: 68.8 us -> none  [the longest x16 45 us: extended(): lax.ppermute(lax.slice_in_dim(block, block.shape[dim] - width, None, axis...]
    psum x1 -> x0, blocking collectives: 65 us -> none  [on_device(): lax.psum((grad_kernel, grad_gate, grad_cand, grad_recur, grad_down), ('ra...]
    dot_general x52 -> x0, matrix products: 62.9 us -> none  [the longest x18 24.8 us: back_product(): lax.dot_general(weight, grads, (((0,), (0,)), ((), ())), preferred_elemen...]
    pallas_call x0 -> x1, Pallas kernels: none -> 60.8 us  [on_device(): pl.pallas_call(functools.partial(kernel, nr, na, scale), out_shape=(jax.S...]
    reshape x15 -> x0, local copies, waits for them, and re-layouts: 32 us -> none  [the longest x4 11.6 us: unpatches(): grads.reshape(channels, 4, 4, tile_rows // 4, tile_cols // 4)]
    transpose x8 -> x0, local copies, waits for them, and re-layouts: 25 us -> none  [the longest x4 13.9 us: patches(): values.reshape(channels, tile_rows // 4, 4, tile_cols // 4, 4)]
  transfers between devices with their start and end apart: 36 -> 0, of which waited for: 12 -> 0; matrix products, arithmetic and copies ran while one was open for 26% -> 0% of each run, Pallas kernels for 0% -> 0%
where the time goes in v1:
time: 70.2 us; the launch traced here: 69.9 us
  Pallas kernels  60.8 us (87%)
  local copies, waits for them, and re-layouts  8.44 us (12%)
    pallas_call x1, Pallas kernels, on_device(): pl.pallas_call(functools.partial(kernel, nr, na, scale), out_shape=(jax.S...  60.8 us
    unnamed x20, local copies, waits for them, and re-layouts  8.44 us

profile of v1, /device:TPU:1, one launch (start us, length us, event | category | flops | bytes accessed | tf_op | source)
XLA Modules:
  0.0 69.9 jit_solution(15701701699724669149)
XLA Ops:
  0.6 60.8 %section.1 = (f32[4,128,128]{2,1,0:T(8,128)}, bf16[4096,128]{1,0:T(8,128)(2,1)}, f32[1024,128]{1,0:T(8,128)}, f32[3,3,64]{2,1,0:T(4,128)}, f32[128,128]{1,0:T(8,...) custom-call(bf16[4096,128]{1,0:T(8,128)(2,1)} %bitcast.8, bf16[1024,128]{1,0:T(8,128)(2,1)} %bitcast.12, ...), custom_call_target="tpu_custom_call" | custom-call | tf_op jit(solution)/shard_map/section/pallas_call | solution.py:714
  61.4 1.7 %copy.26 = f32[1,1,4,128,128]{4,3,2,1,0:T(8,128)} copy(f32[1,1,4,128,128]{4,3,2,1,0:T(8,128)} %bitcast.11) | data formatting | bytes 524288
  63.1 0.0 copy-start.1
  63.1 2.4 %copy.27 = bf16[4,64,16,128]{3,2,1,0:T(8,128)(2,1)} copy(bf16[4,64,16,128]{3,2,1,0:T(8,128)(2,1)} %bitcast.9) | data formatting | bytes 2097152
  65.5 0.0 copy-done.1
  65.5 0.0 copy-start.5
  65.5 0.0 copy-start.2
  65.5 0.0 copy-start
  65.5 0.8 %copy.28 = f32[64,16,128]{2,1,0:T(8,128)} copy(f32[64,16,128]{2,1,0:T(8,128)S(1)} %bitcast.10) | data formatting | bytes 1048576
  66.3 0.0 copy-done.5
  66.3 0.6 copy.29
  66.9 0.0 copy-done.2
  66.9 0.0 copy-start.4
  66.9 0.6 copy.30
  67.6 0.1 copy-done.4
  67.7 0.0 copy-start.3
  67.7 0.6 copy.31
  68.3 0.2 copy-done.3
  68.5 0.6 copy.32
  69.1 0.0 copy-done
  69.1 0.8 %copy.33 = f32[128,1024]{1,0:T(8,128)} copy(f32[128,1024]{1,0:T(8,128)S(1)} %copy-done) | data formatting | bytes 1048576
Async XLA Ops:
  63.1 2.4 %copy-start.1 = (f32[1024,128]{1,0:T(8,128)S(1)}, f32[1024,128]{1,0:T(8,128)}, u32[]{:S(2)}) copy-start(f32[1024,128]{1,0:T(8,128)} %get-tuple-element.18) | copy-start | bytes 1572868
  65.5 0.8 %copy-start.5 = (f32[3,3,64]{2,1,0:T(4,128)S(1)}, f32[3,3,64]{2,1,0:T(4,128)}, u32[]{:S(2)}) copy-start(f32[3,3,64]{2,1,0:T(4,128)} %get-tuple-element.19) | copy-start | bytes 6916
  65.5 1.4 %copy-start.2 = (f32[128,128]{1,0:T(8,128)S(1)}, f32[128,128]{1,0:T(8,128)}, u32[]{:S(2)}) copy-start(f32[128,128]{1,0:T(8,128)} %get-tuple-element.36) | copy-start | bytes 196612
  65.5 3.5 %copy-start = (f32[128,1024]{1,0:T(8,128)S(1)}, f32[128,1024]{1,0:T(8,128)}, u32[]{:S(2)}) copy-start(f32[128,1024]{1,0:T(8,128)} %get-tuple-element.39) | copy-start | bytes 1572868
  66.9 0.8 %copy-start.4 = (f32[64,64]{1,0:T(8,128)S(1)}, f32[64,64]{1,0:T(8,128)}, u32[]{:S(2)}) copy-start(f32[64,64]{1,0:T(8,128)} %get-tuple-element.37) | copy-start | bytes 49156
  67.7 0.8 %copy-start.3 = (f32[64,64]{1,0:T(8,128)S(1)}, f32[64,64]{1,0:T(8,128)}, u32[]{:S(2)}) copy-start(f32[64,64]{1,0:T(8,128)} %get-tuple-element.38) | copy-start | bytes 49156

commit v2 on v1

--- a/solution.py
+++ b/solution.py
@@ -51,16 +51,16 @@
     nr,
     na,
     scale,
-    feat,
-    state,
-    kern,
-    gate,
-    cand,
-    recur,
-    down,
+    feat_in,
+    state_in,
+    kern_in,
+    gate_in,
+    cand_in,
+    recur_in,
+    down_in,
     owner,
     dest,
-    cot,
+    cot_in,
     cart,
     gfeat,
     gstate,
@@ -69,6 +69,12 @@
     gcand,
     grecur,
     gdown,
+    feat,
+    state,
+    kern,
+    cand,
+    recur,
+    down,
     fx,
     xs,
     stk,
@@ -95,7 +101,6 @@
     dwacc,
     gkacc,
     gd,
-    coracc,
     row_s,
     row_r,
     col_s,
@@ -115,6 +120,7 @@
     sm2,
     sm2r,
     sm3,
+    in_sem,
     halo_ss,
     halo_rs,
     cot_ss,
@@ -171,6 +177,24 @@
     lax.fori_loop(1, n2, greet_xy, 0)
     lax.fori_loop(1, n1, greet_z, 0)
 
+    fetches = [
+        pltpu.make_async_copy(src, dst, in_sem.at[n])
+        for n, (src, dst) in enumerate(
+            (
+                (feat_in, feat),
+                (state_in, state),
+                (kern_in, kern),
+                (gate_in, wall.at[pl.ds(0, 2 * CH)]),
+                (cand_in, cand),
+                (recur_in, recur),
+                (down_in, down),
+                (cot_in, cot_all.at[r]),
+            )
+        )
+    ]
+    for fetch in fetches:
+        fetch.start()
+
     lane = iota((GROUP, NCOL), 1)
     lane8 = lane // 8
     lane16 = lane // 16
@@ -185,28 +209,31 @@
         return dcv[t, chans(g), pl.ds(i * NCOL, NCOL)]
 
     def pack(ph, row):
-        def step(n, c):
-            t, g = n // 4, n % 4
+        def step(g, c):
             cs = chans(g)
-            left = jnp.zeros((GROUP, NCOL), F32)
-            right = jnp.zeros((GROUP, NCOL), F32)
-            for i in range(NROW):
-                x = row(t, g, i)
-                y = pltpu.roll(x, (8 * i + 8) % NCOL, 1)
-                right = jnp.where(lane8 == i, y, right)
-                left = jnp.where(lane8 == (i + 1) % 16, y, left)
-                if i in (0, NROW - 1):
-                    end = 0 if i == 0 else 1
-                    row_s[ph, end, t, cs, :] = x.astype(BF16)
-                    spot = 2 * t + end
-                    y = pltpu.roll(x, (16 * spot + 8) % NCOL, 1)
-                    coracc[cs, :] = jnp.where(lane16 == spot, y, coracc[cs, :])
-            col_s[ph, 0, t, cs, :] = pltpu.roll(left, NCOL - 16, 1).astype(BF16)
-            col_s[ph, 1, t, cs, :] = right.astype(BF16)
+            corner = jnp.zeros((GROUP, NCOL), F32)
+            for t in range(NT):
+                left = jnp.zeros((GROUP, NCOL), F32)
+                right = jnp.zeros((GROUP, NCOL), F32)
+                for i in range(NROW):
+                    x = row(t, g, i)
+                    y = pltpu.roll(x, 8 * i + 8, 1) if i < NROW - 1 else x
+                    right = jnp.where(lane8 == i, y, right)
+                    left = jnp.where(lane8 == (i + 1) % 16, y, left)
+                    if i == 0:
+                        row_s[ph, 0, t, cs, :] = x.astype(BF16)
+                        y = pltpu.roll(x, 32 * t + 8, 1)
+                        corner = jnp.where(lane16 == 2 * t, y, corner)
+                    if i == NROW - 1:
+                        row_s[ph, 1, t, cs, :] = x.astype(BF16)
+                        y = pltpu.roll(x, (32 * t + 24) % NCOL, 1)
+                        corner = jnp.where(lane16 == 2 * t + 1, y, corner)
+                col_s[ph, 0, t, cs, :] = pltpu.roll(left, NCOL - 16, 1).astype(BF16)
+                col_s[ph, 1, t, cs, :] = right.astype(BF16)
+            cor_s[ph, cs, :] = corner.astype(BF16)
             return c
 
-        lax.fori_loop(0, 4 * NT, step, 0)
-        cor_s[ph] = coracc[...].astype(BF16)
+        lax.fori_loop(0, 4, step, 0)
 
     def halo_copies(ph):
         copies = []
@@ -288,8 +315,8 @@
         fx[at, :] = feat[at, :].astype(F32)
         return c
 
+    fetches[0].wait()
     lax.fori_loop(0, NT * NAT // 256, widen, 0)
-    coracc[...] = jnp.zeros((CH, NCOL), F32)
     pack(0, feature_row)
     key_row = iota((8, NCOL), 0)
     keys = jnp.zeros((8, NCOL), I32)
@@ -309,11 +336,10 @@
         key_copies.append(
             remote(key_all.at[r], key_all.at[r], key_ss.at[d - 1], key_rs.at[d - 1], device)
         )
-        cot_copies.append(remote(cot, cot_all.at[r], cot_ss.at[d - 1], cot_rs.at[d - 1], device))
-    for copy in cot_copies + key_copies:
-        copy.start()
-
-    cot_all[r] = cot[...]
+        cot_copies.append(
+            remote(cot_all.at[r], cot_all.at[r], cot_ss.at[d - 1], cot_rs.at[d - 1], device)
+        )
+
 
     def make_perm(n, c):
         at = pl.multiple_of(n * 128, 128)
@@ -336,7 +362,10 @@
     spread[...] = (iota((128, SPAN), 0) == (dst // 128) * 32 + (dst % 128) // 4).astype(F32).astype(BF16)
 
     place = iota((CH, 2 * CH), 1) - iota((CH, 2 * CH), 0)
-    wall[0 : 2 * CH, :] = gate[...]
+    for fetch in fetches[1:]:
+        fetch.wait()
+    for copy in cot_copies + key_copies:
+        copy.start()
     wall[2 * CH : 3 * CH, :] = nn(cand[...], (place == 0).astype(F32).astype(BF16)).astype(BF16)
     wall[3 * CH : 4 * CH, :] = nn(recur[...], (place == CH).astype(F32).astype(BF16)).astype(BF16)
     wall_t[...] = wall[...].astype(F32).T.astype(BF16)
@@ -507,10 +536,7 @@
 
     def big_third():
         wait_all(n1, big2)
-        total = sum_slots(gd2[...], gd2r, n1 - 1) * scale
-        gd3[k2] = jnp.concatenate(
-            [total[j * own_rows : (j + 1) * own_rows] for j in range(parts)], axis=1
-        )
+        gd3[k2] = (sum_slots(gd2[...], gd2r, n1 - 1) * scale).astype(BF16)
         start_all(n2, big3)
 
     carry[...] = jnp.zeros(carry.shape, F32)
@@ -546,11 +572,12 @@
             return c2
 
         lax.fori_loop(0, 4, kernel_grad, 0)
-        pl.when(n == 1)(big_second)
-        pl.when(n == 3)(big_third)
-        return c
-
-    lax.fori_loop(0, NT, backward, 0)
+        if n == 2:
+            big_second()
+        return c
+
+    for n in range(NT):
+        backward(n, 0)
 
     lanes = iota((CH, NCOL), 1)
     sm1s[0 : 2 * CH, :] = dwacc[0 : 2 * CH, :]
@@ -563,7 +590,6 @@
     sm1s[3 * CH : 4 * CH, :] = columns
     start_all(n2, small1)
 
-    coracc[...] = jnp.zeros((CH, NCOL), F32)
     pack(1, dconv_row)
     halo1 = halo_copies(1)
     for copy in halo1:
@@ -594,6 +620,7 @@
         return c
 
     lax.fori_loop(0, 4, gather_blocks, 0)
+    big_third()
 
     wait_all(n1, small2)
     sm3[k2] = sum_slots(sm2[...], sm2r, n1 - 1) * scale
@@ -617,7 +644,12 @@
     lax.fori_loop(0, 4 * NT, conv_backward, 0)
 
     wait_all(n2, big3)
-    gdown[...] = gd3[...].reshape(CO, 16 * CH)
+    for k in range(n2):
+        mine = gd3[k].astype(F32)
+        for j in range(parts):
+            gdown[k * own_rows : (k + 1) * own_rows, j * fold_cols : (j + 1) * fold_cols] = mine[
+                j * own_rows : (j + 1) * own_rows
+            ]
 
     wait_all(n2, small3)
     small = sm3[...].reshape(4 * CH, NCOL)
@@ -637,6 +669,17 @@
     sent_all(n2, small1)
     sent_all(n1, small2)
     sent_all(n2, small3)
+
+
+def publish(*refs):
+    count = (len(refs) - 1) // 2
+    copies = [
+        pltpu.make_async_copy(refs[n], refs[count + n], refs[-1].at[n]) for n in range(count)
+    ]
+    for copy in copies:
+        copy.start()
+    for copy in copies:
+        copy.wait()
 
 
 def on_device(nr, na, *args):
@@ -649,9 +692,16 @@
     sm_rows = 4 * CH // n2
     vmem = pl.BlockSpec(memory_space=pltpu.VMEM)
     smem = pl.BlockSpec(memory_space=pltpu.SMEM)
+    hbm = pl.BlockSpec(memory_space=pltpu.HBM)
     dma = pltpu.SemaphoreType.DMA
     cells = (NT, CH, CELLS)
     scratch = [
+        pltpu.VMEM((NT * NAT, NCOL), BF16),
+        pltpu.VMEM((NAT, NCOL), BF16),
+        pltpu.VMEM((3, 3, CH), F32),
+        pltpu.VMEM((CH, CH), BF16),
+        pltpu.VMEM((CH, CH), BF16),
+        pltpu.VMEM((CO, 16 * CH), BF16),
         pltpu.VMEM((NT * NAT, NCOL), F32),
         pltpu.VMEM((NT, 3, NROW + 2, CH, NCOL), F32),
         pltpu.VMEM((NT, 2 * CH, CELLS), BF16),
@@ -678,7 +728,6 @@
         pltpu.VMEM((4 * CH, 2 * CH), F32),
         pltpu.VMEM((9, CH, NCOL), F32),
         pltpu.VMEM((CO, 16 * CH), F32),
-        pltpu.VMEM((CH, NCOL), F32),
         pltpu.VMEM((2, 2, NT, CH, NCOL), BF16),
         pltpu.VMEM((2, 2, NT, CH, NCOL), BF16),
         pltpu.VMEM((2, 2, NT, CH, NCOL), BF16),
@@ -692,12 +741,13 @@
         pltpu.VMEM((n2 - 1, *fold), BF16),
         pltpu.VMEM(fold, F32),
         pltpu.VMEM((n1 - 1, *fold), F32),
-        pltpu.VMEM((n2, own_rows, 16 * CH), F32),
+        pltpu.VMEM((n2, *fold), BF16),
         pltpu.VMEM((4 * CH, NCOL), F32),
         pltpu.VMEM((n2 - 1, sm_rows, NCOL), F32),
         pltpu.VMEM((sm_rows, NCOL), F32),
         pltpu.VMEM((n1 - 1, sm_rows, NCOL), F32),
         pltpu.VMEM((n2, sm_rows, NCOL), F32),
+        dma((8,)),
         dma((2, 8)),
         dma((2, 8)),
         dma((nr - 1,)),
@@ -711,23 +761,24 @@
         dma((2, n1 - 1)),
         dma((2, n1 - 1)),
     ]
+    results = (
+        jax.ShapeDtypeStruct((NT, CO, 128), F32),
+        jax.ShapeDtypeStruct((NT * NAT, NCOL), BF16),
+        jax.ShapeDtypeStruct((NAT, NCOL), F32),
+        jax.ShapeDtypeStruct((3, 3, CH), F32),
+        jax.ShapeDtypeStruct((2 * CH, 2 * CH), F32),
+        jax.ShapeDtypeStruct((CH, CH), F32),
+        jax.ShapeDtypeStruct((CH, CH), F32),
+        jax.ShapeDtypeStruct((CO, 16 * CH), F32),
+    )
     out = pl.pallas_call(
         functools.partial(kernel, nr, na, scale),
-        out_shape=(
-            jax.ShapeDtypeStruct((NT, CO, 128), F32),
-            jax.ShapeDtypeStruct((NT * NAT, NCOL), BF16),
-            jax.ShapeDtypeStruct((NAT, NCOL), F32),
-            jax.ShapeDtypeStruct((3, 3, CH), F32),
-            jax.ShapeDtypeStruct((2 * CH, 2 * CH), F32),
-            jax.ShapeDtypeStruct((CH, CH), F32),
-            jax.ShapeDtypeStruct((CH, CH), F32),
-            jax.ShapeDtypeStruct((CO, 16 * CH), F32),
-        ),
-        in_specs=[vmem] * 7 + [smem] * 2 + [vmem],
+        out_shape=tuple(pltpu.VMEM(x.shape, x.dtype) for x in results),
+        in_specs=[hbm] * 7 + [smem] * 2 + [hbm],
         out_specs=(vmem,) * 8,
         scratch_shapes=scratch,
         compiler_params=pltpu.CompilerParams(
-            collective_id=0, has_side_effects=True, vmem_limit_bytes=60 * 1024 * 1024
+            collective_id=0, has_side_effects=True, vmem_limit_bytes=52 * 1024 * 1024
         ),
         name="section",
     )(
@@ -742,7 +793,15 @@
         dest_map,
         cart_cot.reshape(NT, CO, 128),
     )
-    cart, gfeat, gstate, gkern, ggate, gcand, grecur, gdown = out
+    cart, gfeat, gstate, gkern, ggate, gcand, grecur, gdown = pl.pallas_call(
+        publish,
+        out_shape=results,
+        in_specs=[vmem] * 8,
+        out_specs=(pl.BlockSpec(memory_space=pl.ANY),) * 8,
+        scratch_shapes=[dma((8,))],
+        compiler_params=pltpu.CompilerParams(vmem_limit_bytes=1024 * 1024),
+        name="publish",
+    )(*(pltpu.with_memory_space_constraint(x, pltpu.VMEM) for x in out))
     return (
         cart.reshape(1, 1, NT, CO, 128),
         gfeat.reshape(NT, CH, NROW, NCOL),

time: 70.2 us -> 53.9 us (0.77)
  local copies, waits for them, and re-layouts: 8.44 us -> 0 us
  Pallas kernels: 60.8 us -> 53.1 us
    unnamed x20 -> x0, local copies, waits for them, and re-layouts: 8.44 us -> none
    pallas_call x1 -> x2, Pallas kernels: 60.8 us -> 53.1 us  [the longest x1 51.6 us: on_device(): pl.pallas_call(functools.partial(kernel, nr, na, scale), out_shape=tuple(...]
where the time goes in v2:
time: 53.9 us; the launch traced here: 53.7 us
  Pallas kernels  53.1 us (99%)
  between operations  0.64 us (1%)
    pallas_call x1, Pallas kernels, on_device(): pl.pallas_call(functools.partial(kernel, nr, na, scale), out_shape=tuple(...  51.6 us
    pallas_call x1, Pallas kernels, on_device(): pl.pallas_call(publish, out_shape=results, in_specs=[vmem] * 8, out_specs...  1.52 us

profile of v2, /device:TPU:1, one launch (start us, length us, event | category | flops | bytes accessed | tf_op | source)
XLA Modules:
  0.0 53.7 jit_solution(7120205729198663607)
XLA Ops:
  0.6 51.6 %section.1 = (f32[4,128,128]{2,1,0:T(8,128)S(1)}, bf16[4096,128]{1,0:T(8,128)(2,1)S(1)}, f32[1024,128]{1,0:T(8,128)S(1)}, f32[3,3,64]{2,1,0:T(4,128)S(1)}, f32[1...) custom-call(bf16[4096,128]{1,0:T(8,128)(2,1)} %bitcast.8, ...), custom_call_target="tpu_custom_call" | custom-call | tf_op jit(solution)/shard_map/section/pallas_call | solution.py:774
  52.2 1.5 %publish.1 = (f32[4,128,128]{2,1,0:T(8,128)}, bf16[4096,128]{1,0:T(8,128)(2,1)}, f32[1024,128]{1,0:T(8,128)}, f32[3,3,64]{2,1,0:T(4,128)}, f32[128,128]{1,0:T(8,...) custom-call(f32[4,128,128]{2,1,0:T(8,128)S(1)} %get-tuple-element.24.refs_0_, ...), custom_call_target="tpu_custom_call" | custom-call | tf_op jit(solution)/shard_map/publish/pallas_call | solution.py:796

commit v3 on v2

--- a/solution.py
+++ b/solution.py
@@ -166,22 +166,17 @@
     for dr, da in diagonals:
         greet((ring_r(dr), ring_a(da)))
 
-    def greet_xy(d, c):
+    for d in range(1, n2):
         greet(xy_device(d))
-        return c
-
-    def greet_z(d, c):
+    for d in range(1, n1):
         greet(z_device(d))
-        return c
-
-    lax.fori_loop(1, n2, greet_xy, 0)
-    lax.fori_loop(1, n1, greet_z, 0)
 
     fetches = [
         pltpu.make_async_copy(src, dst, in_sem.at[n])
         for n, (src, dst) in enumerate(
             (
-                (feat_in, feat),
+                (feat_in.at[pl.ds(0, NAT)], feat.at[pl.ds(0, NAT)]),
+                (feat_in.at[pl.ds(NAT, (NT - 1) * NAT)], feat.at[pl.ds(NAT, (NT - 1) * NAT)]),
                 (state_in, state),
                 (kern_in, kern),
                 (gate_in, wall.at[pl.ds(0, 2 * CH)]),
@@ -208,11 +203,11 @@
     def dconv_row(t, g, i):
         return dcv[t, chans(g), pl.ds(i * NCOL, NCOL)]
 
-    def pack(ph, row):
+    def pack(ph, batch, slices, row):
         def step(g, c):
             cs = chans(g)
             corner = jnp.zeros((GROUP, NCOL), F32)
-            for t in range(NT):
+            for t in slices:
                 left = jnp.zeros((GROUP, NCOL), F32)
                 right = jnp.zeros((GROUP, NCOL), F32)
                 for i in range(NROW):
@@ -230,21 +225,22 @@
                         corner = jnp.where(lane16 == 2 * t + 1, y, corner)
                 col_s[ph, 0, t, cs, :] = pltpu.roll(left, NCOL - 16, 1).astype(BF16)
                 col_s[ph, 1, t, cs, :] = right.astype(BF16)
-            cor_s[ph, cs, :] = corner.astype(BF16)
+            cor_s[batch, cs, :] = corner.astype(BF16)
             return c
 
         lax.fori_loop(0, 4, step, 0)
 
-    def halo_copies(ph):
+    def halo_copies(ph, batch, first, count):
         copies = []
+        some = pl.ds(first, count)
         for end, d in ((0, -1), (1, 1)):
             n = len(copies)
             copies.append(
                 remote(
-                    row_s.at[ph, end],
-                    row_r.at[ph, 1 - end],
-                    halo_ss.at[ph, n],
-                    halo_rs.at[ph, n],
+                    row_s.at[ph, end, some],
+                    row_r.at[ph, 1 - end, some],
+                    halo_ss.at[batch, n],
+                    halo_rs.at[batch, n],
                     (ring_r(d), a),
                 )
             )
@@ -252,10 +248,10 @@
             n = len(copies)
             copies.append(
                 remote(
-                    col_s.at[ph, end],
-                    col_r.at[ph, 1 - end],
-                    halo_ss.at[ph, n],
-                    halo_rs.at[ph, n],
+                    col_s.at[ph, end, some],
+                    col_r.at[ph, 1 - end, some],
+                    halo_ss.at[batch, n],
+                    halo_rs.at[batch, n],
                     (r, ring_a(d)),
                 )
             )
@@ -263,10 +259,10 @@
             n = len(copies)
             copies.append(
                 remote(
-                    cor_s.at[ph],
-                    cor_r.at[ph, 3 - j],
-                    halo_ss.at[ph, n],
-                    halo_rs.at[ph, n],
+                    cor_s.at[batch],
+                    cor_r.at[batch, 3 - j],
+                    halo_ss.at[batch, n],
+                    halo_rs.at[batch, n],
                     (ring_r(dr), ring_a(da)),
                 )
             )
@@ -275,7 +271,7 @@
     has_low = (r > 0).astype(F32)
     has_high = (r < nr - 1).astype(F32)
 
-    def windows(ph, row, t, g):
+    def windows(ph, batch, row, t, g):
         cs = chans(g)
         halo_l = col_r[ph, 0, t, cs, :].astype(F32)
         halo_h = col_r[ph, 1, t, cs, :].astype(F32)
@@ -294,8 +290,8 @@
             keep = has_low if end == 0 else has_high
             spot = 2 * t + (1 - end)
             x = row_r[ph, end, t, cs, :].astype(F32) * keep
-            c_l = cor_r[ph, 2 * end, cs, :].astype(F32) * keep
-            c_h = cor_r[ph, 2 * end + 1, cs, :].astype(F32) * keep
+            c_l = cor_r[batch, 2 * end, cs, :].astype(F32) * keep
+            c_h = cor_r[batch, 2 * end + 1, cs, :].astype(F32) * keep
             low = pltpu.roll(c_l, lax.rem(NCOL - 16 * spot, NCOL), 1)
             high = pltpu.roll(c_h, 112 - 16 * spot, 1)
             put(0 if end == 0 else NROW + 1, x, low, high)
@@ -315,20 +311,26 @@
         fx[at, :] = feat[at, :].astype(F32)
         return c
 
-    fetches[0].wait()
-    lax.fori_loop(0, NT * NAT // 256, widen, 0)
-    pack(0, feature_row)
     key_row = iota((8, NCOL), 0)
     keys = jnp.zeros((8, NCOL), I32)
     for b in range(NT):
         keys = jnp.where(key_row == b, owner[0, 0, b] * NT + dest[0, 0, b], keys)
     key_all[r] = keys
 
+    fetches[0].wait()
+    lax.fori_loop(0, NAT // 256, widen, 0)
+    pack(0, 0, [0], feature_row)
     pl.semaphore_wait(barrier, 6 + (n2 - 1) + (n1 - 1))
-
-    halo0 = halo_copies(0)
-    for copy in halo0:
+    first_halo = halo_copies(0, 0, 0, 1)
+    for copy in first_halo:
         copy.start()
+    fetches[1].wait()
+    lax.fori_loop(NAT // 256, NT * NAT // 256, widen, 0)
+    pack(0, 1, list(range(1, NT)), feature_row)
+    rest_halo = halo_copies(0, 1, 1, NT - 1)
+    for copy in rest_halo:
+        copy.start()
+
     cot_copies = []
     key_copies = []
     for d in range(1, nr):
@@ -362,7 +364,7 @@
     spread[...] = (iota((128, SPAN), 0) == (dst // 128) * 32 + (dst % 128) // 4).astype(F32).astype(BF16)
 
     place = iota((CH, 2 * CH), 1) - iota((CH, 2 * CH), 0)
-    for fetch in fetches[1:]:
+    for fetch in fetches[2:]:
         fetch.wait()
     for copy in cot_copies + key_copies:
         copy.start()
@@ -380,13 +382,10 @@
     for i in range(NROW):
         hs[0, :, i * NCOL : (i + 1) * NCOL] = gstate[pl.ds(i, CH, stride=NROW), :]
 
-    for copy in halo0:
-        copy.wait_recv()
-
-    def conv_forward(n, c):
+    def conv_forward(batch, n, c):
         t, g = n // 4, n % 4
         cs = chans(g)
-        shifted = windows(0, feature_row, t, g)
+        shifted = windows(0, batch, feature_row, t, g)
         for b in range(3):
             for i in range(NROW + 2):
                 xs[t, b, i, cs, :] = shifted[b][i]
@@ -396,8 +395,6 @@
 
         convolve(shifted, g, False, store)
         return c
-
-    lax.fori_loop(0, 4 * NT, conv_forward, 0)
 
     def forward(t, c):
         for ic in range(4):
@@ -429,8 +426,30 @@
         blk_all[r, t] = nn(wp[...], pt[t]).astype(BF16)
         return c
 
-    for t in range(NT):
+    gd[...] = jnp.zeros(gd.shape, F32)
+    sub = iota((CO, SPAN), 1) % 4
+
+    def coarse_back(t, c):
+        block = cot_all[owner[0, 0, t], dest[0, 0, t]]
+        wide = nn(block, spread[...])
+        each = [jnp.where(sub == q, wide, 0.0).astype(BF16) for q in range(4)]
+        flow_in[t] = nn(wb[...], jnp.concatenate(each, axis=0))
+        gd[...] += nt(block, pt[t])
+        return c
+
+    for copy in first_halo:
+        copy.wait_recv()
+    lax.fori_loop(0, 4, functools.partial(conv_forward, 0), 0)
+    forward(0, 0)
+    for copy in rest_halo:
+        copy.wait_recv()
+    lax.fori_loop(4, 4 * NT, functools.partial(conv_forward, 1), 0)
+    for copy in cot_copies:
+        copy.wait_recv()
+    for t in range(1, NT):
+        coarse_back(t - 1, 0)
         forward(t, 0)
+    coarse_back(NT - 1, 0)
 
     blk_copies = []
     for d in range(1, nr):
@@ -441,103 +460,75 @@
     for copy in blk_copies:
         copy.start()
 
-    for copy in cot_copies:
-        copy.wait_recv()
-    gd[...] = jnp.zeros(gd.shape, F32)
-    sub = iota((CO, SPAN), 1) % 4
-
-    def coarse_back(t, c):
-        block = cot_all[owner[0, 0, t], dest[0, 0, t]]
-        wide = nn(block, spread[...])
-        each = [jnp.where(sub == q, wide, 0.0).astype(BF16) for q in range(4)]
-        flow_in[t] = nn(wb[...], jnp.concatenate(each, axis=0))
-        gd[...] += nt(block, pt[t])
-        return c
-
-    for t in range(NT):
-        coarse_back(t, 0)
-
-    fold_rows, fold_cols = gds.shape[1], gds.shape[2]
+    fold_rows, fold_cols = gd2.shape
     own_rows = CO // n2
     parts = fold_rows // own_rows
     natural = nt(gd[...].astype(BF16), perm[...])
     for k in range(n2):
         mine = natural[k * own_rows : (k + 1) * own_rows]
-        gds[k] = jnp.concatenate(
+        gds[k * fold_rows : (k + 1) * fold_rows] = jnp.concatenate(
             [mine[:, j * fold_cols : (j + 1) * fold_cols] for j in range(parts)], axis=0
         ).astype(BF16)
 
-    def start_all(count, make):
-        def go(d, c):
-            make(d).start()
-            return c
-
-        lax.fori_loop(1, count, go, 0)
-
-    def wait_all(count, make):
-        def go(d, c):
-            make(d).wait_recv()
-            return c
-
-        lax.fori_loop(1, count, go, 0)
-
-    def sent_all(count, make):
-        def go(d, c):
-            make(d).wait_send()
-            return c
-
-        lax.fori_loop(1, count, go, 0)
-
-    def scatter_copy(slot, src, dst):
+    def scatter(slot, src, piece, dst):
         def make(d):
-            to = lax.rem(k2 + d, n2)
-            return remote(
-                src(to), dst.at[d - 1], xy_ss.at[slot, d - 1], xy_rs.at[slot, d - 1], xy_device(d)
-            )
-
-        return make
-
-    def z_copy(slot, src, dst):
+            at = pl.ds(pl.multiple_of(lax.rem(k2 + d, n2) * piece, piece), piece)
+            return remote(src.at[at], dst.at[d - 1], xy_ss.at[slot], xy_rs.at[slot], xy_device(d))
+
+        every = remote(dst, dst, xy_ss.at[slot], xy_rs.at[slot], xy_device(1))
+        return [make(d) for d in range(1, n2)], every
+
+    def along_z(slot, src, dst):
         def make(d):
-            return remote(src, dst.at[d - 1], z_ss.at[slot, d - 1], z_rs.at[slot, d - 1], z_device(d))
-
-        return make
-
-    def gather_copy(slot, buf):
+            return remote(src, dst.at[d - 1], z_ss.at[slot], z_rs.at[slot], z_device(d))
+
+        every = remote(dst, dst, z_ss.at[slot], z_rs.at[slot], z_device(1))
+        return [make(d) for d in range(1, n1)], every
+
+    def gather(slot, buf):
         def make(d):
-            return remote(
-                buf.at[k2], buf.at[k2], xy_ss.at[slot, d - 1], xy_rs.at[slot, d - 1], xy_device(d)
-            )
-
-        return make
-
-    big1 = scatter_copy(0, lambda to: gds.at[to], gdr)
-    big2 = z_copy(0, gd2, gd2r)
-    big3 = gather_copy(1, gd3)
+            return remote(buf.at[k2], buf.at[k2], xy_ss.at[slot], xy_rs.at[slot], xy_device(d))
+
+        rest = buf.at[pl.ds(0, n2 - 1)]
+        every = remote(rest, rest, xy_ss.at[slot], xy_rs.at[slot], xy_device(1))
+        return [make(d) for d in range(1, n2)], every
+
+    def start_all(exchange):
+        for copy in exchange[0]:
+            copy.start()
+
+    def wait_all(exchange):
+        exchange[1].wait_recv()
+
+    def sent_all(exchange):
+        exchange[1].wait_send()
+
+    big1 = scatter(0, gds, fold_rows, gdr)
+    big2 = along_z(0, gd2, gd2r)
+    big3 = gather(1, gd3)
     sm_rows = 4 * CH // n2
-    small1 = scatter_copy(
-        2, lambda to: sm1s.at[pl.ds(pl.multiple_of(to * sm_rows, sm_rows), sm_rows)], sm1r
-    )
-    small2 = z_copy(1, sm2, sm2r)
-    small3 = gather_copy(3, sm3)
+    small1 = scatter(2, sm1s, sm_rows, sm1r)
+    small2 = along_z(1, sm2, sm2r)
+    small3 = gather(3, sm3)
 
     def sum_slots(own, buf, count):
-        def add(d, total):
-            return total + buf[d].astype(F32)
-
-        return lax.fori_loop(0, count, add, own)
-
-    start_all(n2, big1)
+        total = own
+        for d in range(count):
+            total = total + buf[d].astype(F32)
+        return total
+
+    start_all(big1)
 
     def big_second():
-        wait_all(n2, big1)
-        gd2[...] = sum_slots(gds[k2].astype(F32), gdr, n2 - 1)
-        start_all(n1, big2)
+        wait_all(big1)
+        own = gds[pl.ds(pl.multiple_of(k2 * fold_rows, fold_rows), fold_rows), :]
+        gd2[...] = sum_slots(own.astype(F32), gdr, n2 - 1).astype(BF16)
+        start_all(big2)
 
     def big_third():
-        wait_all(n1, big2)
-        gd3[k2] = (sum_slots(gd2[...], gd2r, n1 - 1) * scale).astype(BF16)
-        start_all(n2, big3)
+        wait_all(big2)
+        gd3[k2] = (sum_slots(gd2[...].astype(F32), gd2r, n1 - 1) * scale).astype(BF16)
+        start_all(big3)
 
     carry[...] = jnp.zeros(carry.shape, F32)
     dwacc[...] = jnp.zeros(dwacc.shape, F32)
@@ -588,20 +579,20 @@
     for tap in range(9):
         columns = jnp.where(lanes == tap, jnp.sum(gkacc[tap], axis=1, keepdims=True), columns)
     sm1s[3 * CH : 4 * CH, :] = columns
-    start_all(n2, small1)
-
-    pack(1, dconv_row)
-    halo1 = halo_copies(1)
+    start_all(small1)
+
+    pack(1, 2, list(range(NT)), dconv_row)
+    halo1 = halo_copies(1, 2, 0, NT)
     for copy in halo1:
         copy.start()
 
     for i in range(NROW):
         gstate[pl.ds(i, CH, stride=NROW), :] = carry[:, i * NCOL : (i + 1) * NCOL]
 
-    wait_all(n2, small1)
+    wait_all(small1)
     own = sm1s[pl.ds(pl.multiple_of(k2 * sm_rows, sm_rows), sm_rows), :]
     sm2[...] = sum_slots(own, sm1r, n2 - 1)
-    start_all(n1, small2)
+    start_all(small2)
 
     for copy in key_copies + blk_copies:
         copy.wait_recv()
@@ -622,16 +613,16 @@
     lax.fori_loop(0, 4, gather_blocks, 0)
     big_third()
 
-    wait_all(n1, small2)
+    wait_all(small2)
     sm3[k2] = sum_slots(sm2[...], sm2r, n1 - 1) * scale
-    start_all(n2, small3)
+    start_all(small3)
 
     for copy in halo1:
         copy.wait_recv()
 
     def conv_backward(n, c):
         t, g = n // 4, n % 4
-        shifted = windows(1, dconv_row, t, g)
+        shifted = windows(1, 2, dconv_row, t, g)
 
         def store(i, total):
             fx[pl.ds(t * NAT + g * GROUP * NROW + i, GROUP, stride=NROW), :] = total
@@ -643,7 +634,7 @@
 
     lax.fori_loop(0, 4 * NT, conv_backward, 0)
 
-    wait_all(n2, big3)
+    wait_all(big3)
     for k in range(n2):
         mine = gd3[k].astype(F32)
         for j in range(parts):
@@ -651,7 +642,7 @@
                 j * own_rows : (j + 1) * own_rows
             ]
 
-    wait_all(n2, small3)
+    wait_all(small3)
     small = sm3[...].reshape(4 * CH, NCOL)
     ggate[...] = small[0 : 2 * CH]
     middle = small[2 * CH : 3 * CH]
@@ -661,14 +652,14 @@
     for tap in range(9):
         gkern[tap // 3, tap % 3 : tap % 3 + 1, :] = lines[tap : tap + 1, :]
 
-    for copy in halo0 + halo1 + cot_copies + key_copies + blk_copies:
+    for copy in first_halo + rest_halo + halo1 + cot_copies + key_copies + blk_copies:
         copy.wait_send()
-    sent_all(n2, big1)
-    sent_all(n1, big2)
-    sent_all(n2, big3)
-    sent_all(n2, small1)
-    sent_all(n1, small2)
-    sent_all(n2, small3)
+    sent_all(big1)
+    sent_all(big2)
+    sent_all(big3)
+    sent_all(small1)
+    sent_all(small2)
+    sent_all(small3)
 
 
 def publish(*refs):
@@ -732,34 +723,34 @@
         pltpu.VMEM((2, 2, NT, CH, NCOL), BF16),
         pltpu.VMEM((2, 2, NT, CH, NCOL), BF16),
         pltpu.VMEM((2, 2, NT, CH, NCOL), BF16),
-        pltpu.VMEM((2, CH, NCOL), BF16),
-        pltpu.VMEM((2, 4, CH, NCOL), BF16),
+        pltpu.VMEM((3, CH, NCOL), BF16),
+        pltpu.VMEM((3, 4, CH, NCOL), BF16),
         pltpu.VMEM((nr, NT, CO, 128), BF16),
         pltpu.VMEM((nr, 8, 128), I32),
         pltpu.VMEM((nr, NT, CO, 128), BF16),
-        pltpu.VMEM((n2, *fold), BF16),
+        pltpu.VMEM((n2 * fold[0], fold[1]), BF16),
         pltpu.VMEM((n2 - 1, *fold), BF16),
-        pltpu.VMEM(fold, F32),
-        pltpu.VMEM((n1 - 1, *fold), F32),
+        pltpu.VMEM(fold, BF16),
+        pltpu.VMEM((n1 - 1, *fold), BF16),
         pltpu.VMEM((n2, *fold), BF16),
         pltpu.VMEM((4 * CH, NCOL), F32),
         pltpu.VMEM((n2 - 1, sm_rows, NCOL), F32),
         pltpu.VMEM((sm_rows, NCOL), F32),
         pltpu.VMEM((n1 - 1, sm_rows, NCOL), F32),
         pltpu.VMEM((n2, sm_rows, NCOL), F32),
-        dma((8,)),
-        dma((2, 8)),
-        dma((2, 8)),
+        dma((9,)),
+        dma((3, 8)),
+        dma((3, 8)),
         dma((nr - 1,)),
         dma((nr - 1,)),
         dma((nr - 1,)),
         dma((nr - 1,)),
         dma((nr - 1,)),
         dma((nr - 1,)),
-        dma((4, n2 - 1)),
-        dma((4, n2 - 1)),
-        dma((2, n1 - 1)),
-        dma((2, n1 - 1)),
+        dma((4,)),
+        dma((4,)),
+        dma((2,)),
+        dma((2,)),
     ]
     results = (
         jax.ShapeDtypeStruct((NT, CO, 128), F32),

time: 53.9 us -> 50.7 us (0.941)
  Pallas kernels: 53.1 us -> 49.9 us
    pallas_call x1, Pallas kernels: 51.6 us -> 48.4 us  [on_device(): pl.pallas_call(functools.partial(kernel, nr, na, scale), out_shape=tuple(...]
where the time goes in v3:
time: 50.7 us; the launch traced here: 50.6 us
  Pallas kernels  49.9 us (98%)
  between operations  0.64 us (1%)
    pallas_call x1, Pallas kernels, on_device(): pl.pallas_call(functools.partial(kernel, nr, na, scale), out_shape=tuple(...  48.4 us
    pallas_call x1, Pallas kernels, on_device(): pl.pallas_call(publish, out_shape=results, in_specs=[vmem] * 8, out_specs...  1.52 us

profile of v3, /device:TPU:1, one launch (start us, length us, event | category | flops | bytes accessed | tf_op | source)
XLA Modules:
  0.0 50.6 jit_solution(13206935935021737858)
XLA Ops:
  0.6 48.4 %section.1 = (f32[4,128,128]{2,1,0:T(8,128)S(1)}, bf16[4096,128]{1,0:T(8,128)(2,1)S(1)}, f32[1024,128]{1,0:T(8,128)S(1)}, f32[3,3,64]{2,1,0:T(4,128)S(1)}, f32[1...) custom-call(bf16[4096,128]{1,0:T(8,128)(2,1)} %bitcast.8, ...), custom_call_target="tpu_custom_call" | custom-call | tf_op jit(solution)/shard_map/section/pallas_call | solution.py:765
  49.0 1.5 %publish.1 = (f32[4,128,128]{2,1,0:T(8,128)}, bf16[4096,128]{1,0:T(8,128)(2,1)}, f32[1024,128]{1,0:T(8,128)}, f32[3,3,64]{2,1,0:T(4,128)}, f32[128,128]{1,0:T(8,...) custom-call(f32[4,128,128]{2,1,0:T(8,128)S(1)} %get-tuple-element.24.refs_0_, ...), custom_call_target="tpu_custom_call" | custom-call | tf_op jit(solution)/shard_map/publish/pallas_call | solution.py:787

commit v4 on v3

--- a/solution.py
+++ b/solution.py
@@ -195,6 +195,8 @@
     lane16 = lane // 16
 
     def chans(g):
+        if isinstance(g, int):
+            return pl.ds(g * GROUP, GROUP)
         return pl.ds(pl.multiple_of(g * GROUP, GROUP), GROUP)
 
     def feature_row(t, g, i):
@@ -342,6 +344,10 @@
             remote(cot_all.at[r], cot_all.at[r], cot_ss.at[d - 1], cot_rs.at[d - 1], device)
         )
 
+    fetches[-1].wait()
+    for copy in cot_copies + key_copies:
+        copy.start()
+
 
     def make_perm(n, c):
         at = pl.multiple_of(n * 128, 128)
@@ -364,10 +370,8 @@
     spread[...] = (iota((128, SPAN), 0) == (dst // 128) * 32 + (dst % 128) // 4).astype(F32).astype(BF16)
 
     place = iota((CH, 2 * CH), 1) - iota((CH, 2 * CH), 0)
-    for fetch in fetches[2:]:
+    for fetch in fetches[2:-1]:
         fetch.wait()
-    for copy in cot_copies + key_copies:
-        copy.start()
     wall[2 * CH : 3 * CH, :] = nn(cand[...], (place == 0).astype(F32).astype(BF16)).astype(BF16)
     wall[3 * CH : 4 * CH, :] = nn(recur[...], (place == CH).astype(F32).astype(BF16)).astype(BF16)
     wall_t[...] = wall[...].astype(F32).T.astype(BF16)
@@ -444,12 +448,14 @@
     for copy in rest_halo:
         copy.wait_recv()
     lax.fori_loop(4, 4 * NT, functools.partial(conv_forward, 1), 0)
+    for t in range(1, NT - 1):
+        forward(t, 0)
     for copy in cot_copies:
         copy.wait_recv()
+    coarse_back(0, 0)
+    forward(NT - 1, 0)
     for t in range(1, NT):
-        coarse_back(t - 1, 0)
-        forward(t, 0)
-    coarse_back(NT - 1, 0)
+        coarse_back(t, 0)
 
     blk_copies = []
     for d in range(1, nr):
@@ -562,8 +568,9 @@
                 gkacc[tap, cs, :] = total
             return c2
 
-        lax.fori_loop(0, 4, kernel_grad, 0)
-        if n == 2:
+        for g in range(4):
+            kernel_grad(g, 0)
+        if n == 3:
             big_second()
         return c
 

time: 50.7 us -> 49.8 us (0.982)
  Pallas kernels: 49.9 us -> 49 us
    pallas_call x1, Pallas kernels: 48.4 us -> 47.5 us  [on_device(): pl.pallas_call(functools.partial(kernel, nr, na, scale), out_shape=tuple(...]
where the time goes in v4:
time: 49.8 us; the launch traced here: 49.7 us
  Pallas kernels  49 us (98%)
  between operations  0.64 us (1%)
    pallas_call x1, Pallas kernels, on_device(): pl.pallas_call(functools.partial(kernel, nr, na, scale), out_shape=tuple(...  47.5 us
    pallas_call x1, Pallas kernels, on_device(): pl.pallas_call(publish, out_shape=results, in_specs=[vmem] * 8, out_specs...  1.52 us

profile of v4, /device:TPU:1, one launch (start us, length us, event | category | flops | bytes accessed | tf_op | source)
XLA Modules:
  0.0 49.7 jit_solution(10849179279006702572)
XLA Ops:
  0.6 47.5 %section.1 = (f32[4,128,128]{2,1,0:T(8,128)S(1)}, bf16[4096,128]{1,0:T(8,128)(2,1)S(1)}, f32[1024,128]{1,0:T(8,128)S(1)}, f32[3,3,64]{2,1,0:T(4,128)S(1)}, f32[1...) custom-call(bf16[4096,128]{1,0:T(8,128)(2,1)} %bitcast.8, ...), custom_call_target="tpu_custom_call" | custom-call | tf_op jit(solution)/shard_map/section/pallas_call | solution.py:772
  48.2 1.5 %publish.1 = (f32[4,128,128]{2,1,0:T(8,128)}, bf16[4096,128]{1,0:T(8,128)(2,1)}, f32[1024,128]{1,0:T(8,128)}, f32[3,3,64]{2,1,0:T(4,128)}, f32[128,128]{1,0:T(8,...) custom-call(f32[4,128,128]{2,1,0:T(8,128)S(1)} %get-tuple-element.24.refs_0_, ...), custom_call_target="tpu_custom_call" | custom-call | tf_op jit(solution)/shard_map/publish/pallas_call | solution.py:794

commit v5 on v4

--- a/solution.py
+++ b/solution.py
@@ -469,9 +469,9 @@
     fold_rows, fold_cols = gd2.shape
     own_rows = CO // n2
     parts = fold_rows // own_rows
-    natural = nt(gd[...].astype(BF16), perm[...])
+    sums = gd[...]
     for k in range(n2):
-        mine = natural[k * own_rows : (k + 1) * own_rows]
+        mine = sums[k * own_rows : (k + 1) * own_rows]
         gds[k * fold_rows : (k + 1) * fold_rows] = jnp.concatenate(
             [mine[:, j * fold_cols : (j + 1) * fold_cols] for j in range(parts)], axis=0
         ).astype(BF16)
@@ -533,7 +533,14 @@
 
     def big_third():
         wait_all(big2)
-        gd3[k2] = (sum_slots(gd2[...].astype(F32), gd2r, n1 - 1) * scale).astype(BF16)
+        total = sum_slots(gd2[...].astype(F32), gd2r, n1 - 1) * scale
+        flat = jnp.concatenate(
+            [total[j * own_rows : (j + 1) * own_rows] for j in range(parts)], axis=1
+        )
+        mine = nt(jnp.concatenate([flat] * parts, axis=0).astype(BF16), perm[...])[0:own_rows]
+        gd3[k2] = jnp.concatenate(
+            [mine[:, j * fold_cols : (j + 1) * fold_cols] for j in range(parts)], axis=0
+        ).astype(BF16)
         start_all(big3)
 
     carry[...] = jnp.zeros(carry.shape, F32)

time: 49.8 us -> 48.9 us (0.982)
  Pallas kernels: 49 us -> 48.2 us
    pallas_call x1, Pallas kernels: 47.5 us -> 46.6 us  [on_device(): pl.pallas_call(functools.partial(kernel, nr, na, scale), out_shape=tuple(...]
where the time goes in v5:
time: 48.9 us; the launch traced here: 48.8 us
  Pallas kernels  48.2 us (99%)
  between operations  0.64 us (1%)
    pallas_call x1, Pallas kernels, on_device(): pl.pallas_call(functools.partial(kernel, nr, na, scale), out_shape=tuple(...  46.6 us
    pallas_call x1, Pallas kernels, on_device(): pl.pallas_call(publish, out_shape=results, in_specs=[vmem] * 8, out_specs...  1.52 us

profile of v5, /device:TPU:1, one launch (start us, length us, event | category | flops | bytes accessed | tf_op | source)
XLA Modules:
  0.0 48.8 jit_solution(497114229957012584)
XLA Ops:
  0.6 46.6 %section.1 = (f32[4,128,128]{2,1,0:T(8,128)S(1)}, bf16[4096,128]{1,0:T(8,128)(2,1)S(1)}, f32[1024,128]{1,0:T(8,128)S(1)}, f32[3,3,64]{2,1,0:T(4,128)S(1)}, f32[1...) custom-call(bf16[4096,128]{1,0:T(8,128)(2,1)} %bitcast.8, ...), custom_call_target="tpu_custom_call" | custom-call | tf_op jit(solution)/shard_map/section/pallas_call | solution.py:779
  47.3 1.5 %publish.1 = (f32[4,128,128]{2,1,0:T(8,128)}, bf16[4096,128]{1,0:T(8,128)(2,1)}, f32[1024,128]{1,0:T(8,128)}, f32[3,3,64]{2,1,0:T(4,128)}, f32[128,128]{1,0:T(8,...) custom-call(f32[4,128,128]{2,1,0:T(8,128)S(1)} %get-tuple-element.24.refs_0_, ...), custom_call_target="tpu_custom_call" | custom-call | tf_op jit(solution)/shard_map/publish/pallas_call | solution.py:801
